TPU v7x, 768 devices: a whole 4x8x12 slice. The times are simulated.
768 devices in a mesh: gx: 6 (over z_hi, core), gy: 4 (over x), gz: 32 (over z_lo, y).
Axes of the slice: x: 4, y: 8, z: 12 (z_hi: 3, z_lo: 4; z = z_hi * 4 + z_lo), core: 2. Of those that a mesh axis runs over, the one named last changes fastest.
Arguments:
- orbitals: float32 [32, 192, 48, 96], P(None, 'gz', 'gx', 'gy'), may hold values from -6 to 6
- potential: float32 [192, 48, 96], P('gz', 'gx', 'gy'), may hold values from -2 to 0.5
- projectors: float32 [32, 6, 4, 64, 1152], P('gz', 'gx', 'gy'), may hold values from -0.1875 to 0.1875
- targets: int32 [32, 6, 4, 16], P('gz', 'gx', 'gy'), may hold values from 0 to 215
- coupling: float32 [32, 6, 4, 32], P('gz', 'gx', 'gy'), may hold values from 0.25 to 2
Outputs:
- filtered: float32 [32, 192, 48, 96], P(None, 'gz', 'gx', 'gy')
Inputs may be any that keep to these rules, and one draw needn't show every extreme that they name: `targets`: A target g names atom g % 8 of the domain at offset (g // 72 - 1, g // 24 % 3 - 1, g // 8 % 3 - 1) in z, x, y from the slot's own domain, periodic; an atom may be named by several slots.
All inputs are finite; a program needn't handle non-finite values.
Results may differ from a plain program's by a relative error of at most 0.0001.
Values sent between devices are 32-bit elements; how exact they have to be, the bound alone decides.
A program may use at most 64 MiB of HBM per device.

v0:
```python
import jax
import jax.numpy as jnp
from jax import lax
from jax.sharding import PartitionSpec as P

NPJ = 4
DEGREE = 3


STENCIL = (
    -5369.0 / 1800.0,
    12.0 / 7.0,
    -15.0 / 56.0,
    10.0 / 189.0,
    -1.0 / 112.0,
    2.0 / 1925.0,
    -1.0 / 16632.0,
)
LOWER_EDGE = 2.0
UPPER_EDGE = 16.0
HIGHEST = lax.Precision.HIGHEST


def with_halo(block, sides, width):
    for axis, dim in sides:
        count = lax.axis_size(axis)
        forward = [(i, i + 1) for i in range(count - 1)]
        forward.append((count - 1, 0))
        backward = [(target, source) for source, target in forward]
        low = lax.ppermute(
            lax.slice_in_dim(block, block.shape[dim] - width, None, axis=dim), axis, forward
        )
        high = lax.ppermute(lax.slice_in_dim(block, 0, width, axis=dim), axis, backward)
        block = jnp.concatenate([low, block, high], axis=dim)
    return block


def band_table(length):
    padded_index = lax.broadcasted_iota(jnp.int32, (length + 12, length), 0)
    cell_index = lax.broadcasted_iota(jnp.int32, (length + 12, length), 1)
    offset = jnp.abs(padded_index - 6 - cell_index)
    table = jnp.zeros((length + 12, length), jnp.float32)
    for distance in range(7):
        table = table + jnp.where(offset == distance, STENCIL[distance], 0.0)
    return table


def stencil_sum(values_in, extended):
    along_z = jnp.einsum(
        "nzxy,zw->nwxy", extended[0], band_table(values_in.shape[1]), precision=HIGHEST
    )
    along_x = jnp.einsum(
        "nzxy,xw->nzwy", extended[1], band_table(values_in.shape[2]), precision=HIGHEST
    )
    along_y = jnp.einsum(
        "nzxy,yw->nzxw", extended[2], band_table(values_in.shape[3]), precision=HIGHEST
    )
    return along_z + along_x + along_y


def laplacian(values_in):
    depth_cells = values_in.shape[1]
    width_cells = values_in.shape[2]
    height_cells = values_in.shape[3]
    padded = with_halo(values_in, (("gx", 2), ("gy", 3), ("gz", 1)), 6)
    extended = (
        padded[:, :, 6 : 6 + width_cells, 6 : 6 + height_cells],
        padded[:, 6 : 6 + depth_cells, :, 6 : 6 + height_cells],
        padded[:, 6 : 6 + depth_cells, 6 : 6 + width_cells, :],
    )
    return stencil_sum(values_in, extended)


def nonlocal_term(values_in, projector_rows, selector, weights):
    orbital_count = values_in.shape[0]
    flattened = values_in.reshape(orbital_count, -1)
    partial_value = lax.dot_general(
        projector_rows,
        flattened,
        (((1,), (1,)), ((), ())),
        precision=HIGHEST,
        preferred_element_type=jnp.float32,
    )
    partial_value = partial_value.reshape(selector.shape[1], -1)
    grouped = jnp.dot(
        selector, partial_value, precision=HIGHEST, preferred_element_type=jnp.float32
    )
    entry_width = weights.shape[0] * orbital_count
    grouped = grouped.reshape(3, 3, 3, entry_width)
    padded = with_halo(grouped, (("gx", 1), ("gy", 2), ("gz", 0)), 1)
    summed = jnp.sum(padded[0::2, 0::2, 0::2], axis=(0, 1, 2))
    scaled = (summed.reshape(weights.shape[0], orbital_count) * weights[:, None]).reshape(
        1, 1, 1, entry_width
    )
    beside_all = with_halo(scaled, (("gx", 1), ("gy", 2), ("gz", 0)), 1)
    beside_all = beside_all.reshape(selector.shape[0], -1)
    picked = lax.dot_general(
        selector,
        beside_all,
        (((0,), (0,)), ((), ())),
        precision=HIGHEST,
        preferred_element_type=jnp.float32,
    )
    picked = picked.reshape(-1, orbital_count)
    returned = lax.dot_general(
        picked,
        projector_rows,
        (((0,), (0,)), ((), ())),
        precision=HIGHEST,
        preferred_element_type=jnp.float32,
    )
    return returned.reshape(values_in.shape)


def shards(orbitals, potential, projectors, targets, coupling):
    projector_rows = projectors.reshape(projectors.shape[3], projectors.shape[4])
    slot_targets = targets.reshape(-1)
    weights = coupling.reshape(-1)
    segments = 27 * (weights.shape[0] // NPJ)
    selector = (
        lax.broadcasted_iota(jnp.int32, (segments, slot_targets.shape[0]), 0)
        == slot_targets[None, :]
    ).astype(jnp.float32)
    centre = 0.5 * (UPPER_EDGE + LOWER_EDGE)
    spread = 0.5 * (UPPER_EDGE - LOWER_EDGE)

    def shifted(values_in):
        applied = -0.5 * laplacian(values_in) + potential[None] * values_in
        applied = applied + nonlocal_term(values_in, projector_rows, selector, weights)
        return (applied - centre * values_in) / spread

    previous = orbitals
    current = shifted(orbitals)
    for degree_step in range(1, DEGREE):
        following = 2.0 * shifted(current) - previous
        previous, current = (current, following)
    return current


def solution(mesh):
    return jax.shard_map(
        shards,
        mesh=mesh,
        in_specs=(
            P(None, "gz", "gx", "gy"),
            P("gz", "gx", "gy"),
            P("gz", "gx", "gy", None, None),
            P("gz", "gx", "gy", None),
            P("gz", "gx", "gy", None),
        ),
        out_specs=P(None, "gz", "gx", "gy"),
        check_vma=False,
    )
```

profile of v0, /device:TPU:1, one launch (start us, length us, event | category | flops | bytes accessed | tf_op | source)
XLA Modules:
  0.0 491.7 jit_solution(11720499915013883511)
XLA Ops:
  2.8 12.0 %collective-permute-start.6 = (f32[3,1,3,1024]{3,2,1,0:T(4,128)S(1)}, f32[3,1,3,1024]{3,2,1,0:T(4,128)S(1)}, u32[]{:S(2)}, u32[]{:S(2)}) collective-permute-start(f32[3,1,3,1024]{3,2,1,0:T(4,128)S(1)} %get-tuple-element.34), channel_id=1, source_target_pairs={{0,128},{128,256},{256,384},{384,512},{512,640},{640,0},{1,129},{1... | collective-permute-start | bytes 110600 | tf_op jit(solution)/shard_map/ppermute | solution.py:30
  18.0 7.1 %collective-permute-start = (f32[32,6,6,24]{0,3,2,1:T(8,128)S(1)}, f32[32,6,6,24]{0,3,2,1:T(8,128)}, u32[]{:S(2)}, u32[]{:S(2)}) collective-permute-start(f32[32,6,6,24]{0,3,2,1:T(8,128)S(1)} %get-tuple-element.16), channel_id=1, source_target_pairs={{0,128},{128,256},{256,384},{384,512},{512,640},{640,0},{1,129},{1... | collective-permute-start | bytes 331784 | tf_op jit(solution)/shard_map/ppermute | solution.py:30
  28.1 4.0 collective-permute-start.9
  34.1 4.6 collective-permute-done.8
  38.8 10.2 %collective-permute-start.11 = (f32[1,5,5,1024]{3,2,1,0:T(8,128)S(1)}, f32[1,5,5,1024]{3,2,1,0:T(8,128)S(1)}, u32[]{:S(2)}, u32[]{:S(2)}) collective-permute-start(f32[1,5,5,1024]{3,2,1,0:T(8,128)S(1)} %get-tuple-element.22), channel_id=1, source_target_pairs={{1,0},{2,1},{3,2},{4,3},{5,4},{6,5},{7,6},{8,7},{9,8},{10,9},{11,1... | collective-permute-start | bytes 307208 | tf_op jit(solution)/shard_map/ppermute | solution.py:33
  56.6 3.4 collective-permute-start.2
  62.6 5.1 %slice.129 = f32[3,3,3,1024]{3,2,1,0:T(4,128)} slice(f32[5,5,5,1024]{3,2,1,0:T(8,128)} %pad_maximum_fusion.25), slice={[0:5:2], [0:5:2], [0:5:2], [0:1024:1]} | slice | bytes 221184 | tf_op jit(solution)/shard_map/slice | solution.py:91
  68.7 3.5 collective-permute-start.13
  72.2 6.3 %collective-permute-start.12 = (f32[1,1,1,1024]{3,2,1,0:T(1,128)S(1)}, f32[1,1,1,1024]{3,2,1,0:T(1,128)S(1)}, u32[]{:S(2)}, u32[]{:S(2)}) collective-permute-start(f32[1,1,1,1024]{3,2,1,0:T(1,128)S(1)} %mul.105), channel_id=1, source_target_pairs={{0,128},{128,256},{256,384},{384,512},{512,640},{640,0},{1,129},{1... | collective-permute-start | bytes 12296 | tf_op jit(solution)/shard_map/ppermute | solution.py:30
  81.3 3.3 collective-permute-start.15
  90.8 3.4 copy.125
  94.2 9.0 %collective-permute-start.5 = (f32[32,6,20,36]{3,0,2,1:T(8,128)}, f32[32,6,20,36]{3,0,2,1:T(8,128)}, u32[]{:S(2)}, u32[]{:S(2)}) collective-permute-start(f32[32,6,20,36]{3,0,2,1:T(8,128)} %copy.125), channel_id=1, source_target_pairs={{1,0},{2,1},{3,2},{4,3},{5,4},{6,5},{7,6},{8,7},{9,8},{10,9},{11,1... | collective-permute-start | bytes 1658888 | tf_op jit(solution)/shard_map/ppermute | solution.py:33
  105.2 7.3 %collective-permute-start.17 = (f32[1,3,3,1024]{3,2,1,0:T(4,128)S(1)}, f32[1,3,3,1024]{3,2,1,0:T(4,128)S(1)}, u32[]{:S(2)}, u32[]{:S(2)}) collective-permute-start(f32[1,3,3,1024]{3,2,1,0:T(4,128)S(1)} %pad_maximum_fusion.40), channel_id=1, source_target_pairs={{1,0},{2,1},{3,2},{4,3},{5,4},{6,5},{7,6},{8,7},{9,8},{10,9},{11,1... | collective-permute-start | bytes 110600 | tf_op jit(solution)/shard_map/ppermute | solution.py:33
  117.6 29.3 %collective-permute-done.17 = f32[1,3,3,1024]{3,2,1,0:T(4,128)S(1)} collective-permute-done((f32[1,3,3,1024]{3,2,1,0:T(4,128)S(1)}, f32[1,3,3,1024]{3,2,1,0:T(4,128)S(1)}, u32[]{:S(2)}, u32[]{:S(2)}) %collective-permute-start.17) | collective-permute-done | bytes 36896 | tf_op jit(solution)/shard_map/ppermute | solution.py:33
  146.9 7.8 %collective-permute-done.16 = f32[1,3,3,1024]{3,2,1,0:T(4,128)S(1)} collective-permute-done((f32[1,3,3,1024]{3,2,1,0:T(4,128)S(1)}, f32[1,3,3,1024]{3,2,1,0:T(4,128)S(1)}, u32[]{:S(2)}, u32[]{:S(2)}) %collective-permute-start.16) | collective-permute-done | bytes 36896 | tf_op jit(solution)/shard_map/ppermute | solution.py:30
  158.2 3.6 copy.128
  161.8 3.6 copy.127
  171.9 6.0 %collective-permute-start.24 = (f32[3,1,3,1024]{3,2,1,0:T(4,128)S(1)}, f32[3,1,3,1024]{3,2,1,0:T(4,128)S(1)}, u32[]{:S(2)}, u32[]{:S(2)}) collective-permute-start(f32[3,1,3,1024]{3,2,1,0:T(4,128)S(1)} %get-tuple-element.32), channel_id=1, source_target_pairs={{0,128},{128,256},{256,384},{384,512},{512,640},{640,0},{1,129},{1... | collective-permute-start | bytes 110600 | tf_op jit(solution)/shard_map/ppermute | solution.py:30
  180.5 7.3 %collective-permute-done.25 = f32[3,1,3,1024]{3,2,1,0:T(4,128)S(1)} collective-permute-done((f32[3,1,3,1024]{3,2,1,0:T(4,128)S(1)}, f32[3,1,3,1024]{3,2,1,0:T(4,128)S(1)}, u32[]{:S(2)}, u32[]{:S(2)}) %collective-permute-start.25) | collective-permute-done | bytes 36896 | tf_op jit(solution)/shard_map/ppermute | solution.py:33
  187.9 4.6 collective-permute-start.27
  196.5 7.5 %collective-permute-start.18 = (f32[32,6,6,24]{0,3,2,1:T(8,128)S(1)}, f32[32,6,6,24]{0,3,2,1:T(8,128)S(1)}, u32[]{:S(2)}, u32[]{:S(2)}) collective-permute-start(f32[32,6,6,24]{0,3,2,1:T(8,128)S(1)} %get-tuple-element.13), channel_id=1, source_target_pairs={{0,128},{128,256},{256,384},{384,512},{512,640},{640,0},{1,129},{1... | collective-permute-start | bytes 331784 | tf_op jit(solution)/shard_map/ppermute | solution.py:30
  206.1 3.4 collective-permute-start.28
  209.4 3.7 collective-permute-done.19
  213.1 5.5 %collective-permute-done.18 = f32[32,6,6,24]{0,3,2,1:T(8,128)S(1)} collective-permute-done((f32[32,6,6,24]{0,3,2,1:T(8,128)S(1)}, f32[32,6,6,24]{0,3,2,1:T(8,128)S(1)}, u32[]{:S(2)}, u32[]{:S(2)}) %collective-permute-start.18) | collective-permute-done | bytes 110624 | tf_op jit(solution)/shard_map/ppermute | solution.py:30
  221.4 5.1 %slice.142 = f32[3,3,3,1024]{3,2,1,0:T(4,128)} slice(f32[5,5,5,1024]{3,2,1,0:T(8,128)} %pad_maximum_fusion.26), slice={[0:5:2], [0:5:2], [0:5:2], [0:1024:1]} | slice | bytes 221184 | tf_op jit(solution)/shard_map/slice | solution.py:91
  227.6 5.9 %collective-permute-start.31 = (f32[1,1,1,1024]{3,2,1,0:T(1,128)S(1)}, f32[1,1,1,1024]{3,2,1,0:T(1,128)S(1)}, u32[]{:S(2)}, u32[]{:S(2)}) collective-permute-start(f32[1,1,1,1024]{3,2,1,0:T(1,128)S(1)} %mul.112), channel_id=1, source_target_pairs={{128,0},{256,128},{384,256},{512,384},{640,512},{0,640},{129,1},{2... | collective-permute-start | bytes 12296 | tf_op jit(solution)/shard_map/ppermute | solution.py:33
  233.5 3.7 collective-permute-start.30
  239.8 4.6 collective-permute-start.33
  246.4 4.6 collective-permute-start.21
  253.0 7.7 %collective-permute-start.35 = (f32[1,3,3,1024]{3,2,1,0:T(4,128)S(1)}, f32[1,3,3,1024]{3,2,1,0:T(4,128)S(1)}, u32[]{:S(2)}, u32[]{:S(2)}) collective-permute-start(f32[1,3,3,1024]{3,2,1,0:T(4,128)S(1)} %pad_maximum_fusion.41), channel_id=1, source_target_pairs={{1,0},{2,1},{3,2},{4,3},{5,4},{6,5},{7,6},{8,7},{9,8},{10,9},{11,1... | collective-permute-start | bytes 110600 | tf_op jit(solution)/shard_map/ppermute | solution.py:33
  268.3 7.7 %collective-permute-start.23 = (f32[32,6,20,36]{3,0,2,1:T(8,128)}, f32[32,6,20,36]{3,0,2,1:T(8,128)}, u32[]{:S(2)}, u32[]{:S(2)}) collective-permute-start(f32[32,6,20,36]{3,0,2,1:T(8,128)} %copy.136), channel_id=1, source_target_pairs={{1,0},{2,1},{3,2},{4,3},{5,4},{6,5},{7,6},{8,7},{9,8},{10,9},{11,1... | collective-permute-start | bytes 1658888 | tf_op jit(solution)/shard_map/ppermute | solution.py:33
  280.1 33.7 %collective-permute-done.23 = f32[32,6,20,36]{3,0,2,1:T(8,128)} collective-permute-done((f32[32,6,20,36]{3,0,2,1:T(8,128)}, f32[32,6,20,36]{3,0,2,1:T(8,128)}, u32[]{:S(2)}, u32[]{:S(2)}) %collective-permute-start.23) | collective-permute-done | bytes 552992 | tf_op jit(solution)/shard_map/ppermute | solution.py:33
  317.1 4.5 collective-permute-done.22
  321.6 3.3 copy.138
  331.8 11.5 %collective-permute-start.42 = (f32[3,1,3,1024]{3,2,1,0:T(4,128)S(1)}, f32[3,1,3,1024]{3,2,1,0:T(4,128)S(1)}, u32[]{:S(2)}, u32[]{:S(2)}) collective-permute-start(f32[3,1,3,1024]{3,2,1,0:T(4,128)S(1)} %get-tuple-element.30), channel_id=1, source_target_pairs={{0,128},{128,256},{256,384},{384,512},{512,640},{640,0},{1,129},{1... | collective-permute-start | bytes 110600 | tf_op jit(solution)/shard_map/ppermute | solution.py:30
  345.4 7.3 %collective-permute-done.43 = f32[3,1,3,1024]{3,2,1,0:T(4,128)S(1)} collective-permute-done((f32[3,1,3,1024]{3,2,1,0:T(4,128)S(1)}, f32[3,1,3,1024]{3,2,1,0:T(4,128)S(1)}, u32[]{:S(2)}, u32[]{:S(2)}) %collective-permute-start.43) | collective-permute-done | bytes 36896 | tf_op jit(solution)/shard_map/ppermute | solution.py:33
  360.1 7.5 %collective-permute-start.36 = (f32[32,6,6,24]{0,3,2,1:T(8,128)S(1)}, f32[32,6,6,24]{0,3,2,1:T(8,128)S(1)}, u32[]{:S(2)}, u32[]{:S(2)}) collective-permute-start(f32[32,6,6,24]{0,3,2,1:T(8,128)S(1)} %get-tuple-element.11), channel_id=1, source_target_pairs={{0,128},{128,256},{256,384},{384,512},{512,640},{640,0},{1,129},{1... | collective-permute-start | bytes 331784 | tf_op jit(solution)/shard_map/ppermute | solution.py:30
  367.8 3.4 collective-permute-start.47
  375.4 6.5 %collective-permute-done.36 = f32[32,6,6,24]{0,3,2,1:T(8,128)S(1)} collective-permute-done((f32[32,6,6,24]{0,3,2,1:T(8,128)S(1)}, f32[32,6,6,24]{0,3,2,1:T(8,128)S(1)}, u32[]{:S(2)}, u32[]{:S(2)}) %collective-permute-start.36) | collective-permute-done | bytes 110624 | tf_op jit(solution)/shard_map/ppermute | solution.py:30
  386.9 4.2 slice.155
  393.5 7.2 %collective-permute-start.48 = (f32[1,1,1,1024]{3,2,1,0:T(1,128)S(1)}, f32[1,1,1,1024]{3,2,1,0:T(1,128)S(1)}, u32[]{:S(2)}, u32[]{:S(2)}) collective-permute-start(f32[1,1,1,1024]{3,2,1,0:T(1,128)S(1)} %mul.119), channel_id=1, source_target_pairs={{0,128},{128,256},{256,384},{384,512},{512,640},{640,0},{1,129},{1... | collective-permute-start | bytes 12296 | tf_op jit(solution)/shard_map/ppermute | solution.py:30
  408.1 4.3 collective-permute-start.39
  414.4 5.7 %collective-permute-start.53 = (f32[1,3,3,1024]{3,2,1,0:T(4,128)S(1)}, f32[1,3,3,1024]{3,2,1,0:T(4,128)S(1)}, u32[]{:S(2)}, u32[]{:S(2)}) collective-permute-start(f32[1,3,3,1024]{3,2,1,0:T(4,128)S(1)} %pad_maximum_fusion.42), channel_id=1, source_target_pairs={{1,0},{2,1},{3,2},{4,3},{5,4},{6,5},{7,6},{8,7},{9,8},{10,9},{11,1... | collective-permute-start | bytes 110600 | tf_op jit(solution)/shard_map/ppermute | solution.py:33
  426.4 3.3 copy.148
  429.7 6.3 %collective-permute-start.41 = (f32[32,6,20,36]{3,0,2,1:T(8,128)}, f32[32,6,20,36]{3,0,2,1:T(8,128)}, u32[]{:S(2)}, u32[]{:S(2)}) collective-permute-start(f32[32,6,20,36]{3,0,2,1:T(8,128)} %copy.148), channel_id=1, source_target_pairs={{1,0},{2,1},{3,2},{4,3},{5,4},{6,5},{7,6},{8,7},{9,8},{10,9},{11,1... | collective-permute-start | bytes 1658888 | tf_op jit(solution)/shard_map/ppermute | solution.py:33
  439.3 35.2 %collective-permute-done.41 = f32[32,6,20,36]{3,0,2,1:T(8,128)} collective-permute-done((f32[32,6,20,36]{3,0,2,1:T(8,128)}, f32[32,6,20,36]{3,0,2,1:T(8,128)}, u32[]{:S(2)}, u32[]{:S(2)}) %collective-permute-start.41) | collective-permute-done | bytes 552992 | tf_op jit(solution)/shard_map/ppermute | solution.py:33
  477.8 4.5 collective-permute-done.40
  482.3 3.3 copy.150
  (251 shorter events, 137.5 us)
Async XLA Ops:
  2.8 25.1 %collective-permute-start.6 = (f32[3,1,3,1024]{3,2,1,0:T(4,128)S(1)}, f32[3,1,3,1024]{3,2,1,0:T(4,128)S(1)}, u32[]{:S(2)}, u32[]{:S(2)}) collective-permute-start(f32[3,1,3,1024]{3,2,1,0:T(4,128)S(1)} %get-tuple-element.34), channel_id=1, source_target_pairs={{0,128},{128,256},{256,384},{384,512},{512,640},{640,0},{1,129},{1... | collective-permute-start | bytes 110600 | tf_op jit(solution)/shard_map/ppermute | solution.py:30
  14.8 13.2 %collective-permute-start.7 = (f32[3,1,3,1024]{3,2,1,0:T(4,128)S(1)}, f32[3,1,3,1024]{3,2,1,0:T(4,128)S(1)}, u32[]{:S(2)}, u32[]{:S(2)}) collective-permute-start(f32[3,1,3,1024]{3,2,1,0:T(4,128)S(1)} %get-tuple-element.33), channel_id=1, source_target_pairs={{128,0},{256,128},{384,256},{512,384},{640,512},{0,640},{129,1},{2... | collective-permute-start | bytes 110600 | tf_op jit(solution)/shard_map/ppermute | solution.py:33
  18.0 33.0 %collective-permute-start = (f32[32,6,6,24]{0,3,2,1:T(8,128)S(1)}, f32[32,6,6,24]{0,3,2,1:T(8,128)}, u32[]{:S(2)}, u32[]{:S(2)}) collective-permute-start(f32[32,6,6,24]{0,3,2,1:T(8,128)S(1)} %get-tuple-element.16), channel_id=1, source_target_pairs={{0,128},{128,256},{256,384},{384,512},{512,640},{640,0},{1,129},{1... | collective-permute-start | bytes 331784 | tf_op jit(solution)/shard_map/ppermute | solution.py:30
  25.1 27.4 %collective-permute-start.1 = (f32[32,6,6,24]{0,3,2,1:T(8,128)}, f32[32,6,6,24]{0,3,2,1:T(8,128)}, u32[]{:S(2)}, u32[]{:S(2)}) collective-permute-start(f32[32,6,6,24]{0,3,2,1:T(8,128)} %get-tuple-element.15), channel_id=1, source_target_pairs={{128,0},{256,128},{384,256},{512,384},{640,512},{0,640},{129,1},{2... | collective-permute-start | bytes 331784 | tf_op jit(solution)/shard_map/ppermute | solution.py:33
  38.8 21.2 %collective-permute-start.11 = (f32[1,5,5,1024]{3,2,1,0:T(8,128)S(1)}, f32[1,5,5,1024]{3,2,1,0:T(8,128)S(1)}, u32[]{:S(2)}, u32[]{:S(2)}) collective-permute-start(f32[1,5,5,1024]{3,2,1,0:T(8,128)S(1)} %get-tuple-element.22), channel_id=1, source_target_pairs={{1,0},{2,1},{3,2},{4,3},{5,4},{6,5},{7,6},{8,7},{9,8},{10,9},{11,1... | collective-permute-start | bytes 307208 | tf_op jit(solution)/shard_map/ppermute | solution.py:33
  49.0 12.5 %collective-permute-start.10 = (f32[1,5,5,1024]{3,2,1,0:T(8,128)S(1)}, f32[1,5,5,1024]{3,2,1,0:T(8,128)S(1)}, u32[]{:S(2)}, u32[]{:S(2)}) collective-permute-start(f32[1,5,5,1024]{3,2,1,0:T(8,128)S(1)} %get-tuple-element.21), channel_id=1, source_target_pairs={{0,1},{1,2},{2,3},{3,4},{4,5},{5,6},{6,7},{7,8},{8,9},{9,10},{10,1... | collective-permute-start | bytes 307208 | tf_op jit(solution)/shard_map/ppermute | solution.py:30
  54.7 31.9 %collective-permute-start.3 = (f32[32,6,20,6]{0,1,3,2:T(8,128)}, f32[32,6,20,6]{0,1,3,2:T(8,128)}, u32[]{:S(2)}, u32[]{:S(2)}) collective-permute-start(f32[32,6,20,6]{0,1,3,2:T(8,128)} %get-tuple-element.6), channel_id=1, source_target_pairs={{32,0},{64,32},{96,64},{0,96},{33,1},{65,33},{97,65},{1,97},{34,2}... | collective-permute-start | bytes 276488 | tf_op jit(solution)/shard_map/ppermute | solution.py:33
  56.6 30.0 %collective-permute-start.2 = (f32[32,6,20,6]{0,1,3,2:T(8,128)}, f32[32,6,20,6]{0,1,3,2:T(8,128)}, u32[]{:S(2)}, u32[]{:S(2)}) collective-permute-start(f32[32,6,20,6]{0,1,3,2:T(8,128)} %get-tuple-element.5), channel_id=1, source_target_pairs={{0,32},{32,64},{64,96},{96,0},{1,33},{33,65},{65,97},{97,1},{2,34}... | collective-permute-start | bytes 276488 | tf_op jit(solution)/shard_map/ppermute | solution.py:30
  68.7 12.6 %collective-permute-start.13 = (f32[1,1,1,1024]{3,2,1,0:T(1,128)S(1)}, f32[1,1,1,1024]{3,2,1,0:T(1,128)S(1)}, u32[]{:S(2)}, u32[]{:S(2)}) collective-permute-start(f32[1,1,1,1024]{3,2,1,0:T(1,128)S(1)} %mul.105), channel_id=1, source_target_pairs={{128,0},{256,128},{384,256},{512,384},{640,512},{0,640},{129,1},{2... | collective-permute-start | bytes 12296 | tf_op jit(solution)/shard_map/ppermute | solution.py:33
  72.2 9.0 %collective-permute-start.12 = (f32[1,1,1,1024]{3,2,1,0:T(1,128)S(1)}, f32[1,1,1,1024]{3,2,1,0:T(1,128)S(1)}, u32[]{:S(2)}, u32[]{:S(2)}) collective-permute-start(f32[1,1,1,1024]{3,2,1,0:T(1,128)S(1)} %mul.105), channel_id=1, source_target_pairs={{0,128},{128,256},{256,384},{384,512},{512,640},{640,0},{1,129},{1... | collective-permute-start | bytes 12296 | tf_op jit(solution)/shard_map/ppermute | solution.py:30
  81.3 23.9 %collective-permute-start.15 = (f32[1,3,1,1024]{3,2,1,0:T(1,128)S(1)}, f32[1,3,1,1024]{3,2,1,0:T(1,128)S(1)}, u32[]{:S(2)}, u32[]{:S(2)}) collective-permute-start(f32[1,3,1,1024]{3,2,1,0:T(1,128)S(1)} %pad_maximum_fusion.43), channel_id=1, source_target_pairs={{32,0},{64,32},{96,64},{0,96},{33,1},{65,33},{97,65},{1,97},{34,2}... | collective-permute-start | bytes 36872 | tf_op jit(solution)/shard_map/ppermute | solution.py:33
  84.6 20.6 %collective-permute-start.14 = (f32[1,3,1,1024]{3,2,1,0:T(1,128)S(1)}, f32[1,3,1,1024]{3,2,1,0:T(1,128)S(1)}, u32[]{:S(2)}, u32[]{:S(2)}) collective-permute-start(f32[1,3,1,1024]{3,2,1,0:T(1,128)S(1)} %pad_maximum_fusion.43), channel_id=1, source_target_pairs={{0,32},{32,64},{64,96},{96,0},{1,33},{33,65},{65,97},{97,1},{2,34}... | collective-permute-start | bytes 36872 | tf_op jit(solution)/shard_map/ppermute | solution.py:30
  94.2 64.0 %collective-permute-start.5 = (f32[32,6,20,36]{3,0,2,1:T(8,128)}, f32[32,6,20,36]{3,0,2,1:T(8,128)}, u32[]{:S(2)}, u32[]{:S(2)}) collective-permute-start(f32[32,6,20,36]{3,0,2,1:T(8,128)} %copy.125), channel_id=1, source_target_pairs={{1,0},{2,1},{3,2},{4,3},{5,4},{6,5},{7,6},{8,7},{9,8},{10,9},{11,1... | collective-permute-start | bytes 1658888 | tf_op jit(solution)/shard_map/ppermute | solution.py:33
  103.2 58.6 %collective-permute-start.4 = (f32[32,6,20,36]{3,0,2,1:T(8,128)}, f32[32,6,20,36]{3,0,2,1:T(8,128)}, u32[]{:S(2)}, u32[]{:S(2)}) collective-permute-start(f32[32,6,20,36]{3,0,2,1:T(8,128)} %copy.125), channel_id=1, source_target_pairs={{0,1},{1,2},{2,3},{3,4},{4,5},{5,6},{6,7},{7,8},{8,9},{9,10},{10,1... | collective-permute-start | bytes 1658888 | tf_op jit(solution)/shard_map/ppermute | solution.py:30
  105.2 41.6 %collective-permute-start.17 = (f32[1,3,3,1024]{3,2,1,0:T(4,128)S(1)}, f32[1,3,3,1024]{3,2,1,0:T(4,128)S(1)}, u32[]{:S(2)}, u32[]{:S(2)}) collective-permute-start(f32[1,3,3,1024]{3,2,1,0:T(4,128)S(1)} %pad_maximum_fusion.40), channel_id=1, source_target_pairs={{1,0},{2,1},{3,2},{4,3},{5,4},{6,5},{7,6},{8,7},{9,8},{10,9},{11,1... | collective-permute-start | bytes 110600 | tf_op jit(solution)/shard_map/ppermute | solution.py:33
  112.5 42.2 %collective-permute-start.16 = (f32[1,3,3,1024]{3,2,1,0:T(4,128)S(1)}, f32[1,3,3,1024]{3,2,1,0:T(4,128)S(1)}, u32[]{:S(2)}, u32[]{:S(2)}) collective-permute-start(f32[1,3,3,1024]{3,2,1,0:T(4,128)S(1)} %pad_maximum_fusion.40), channel_id=1, source_target_pairs={{0,1},{1,2},{2,3},{3,4},{4,5},{5,6},{6,7},{7,8},{8,9},{9,10},{10,1... | collective-permute-start | bytes 110600 | tf_op jit(solution)/shard_map/ppermute | solution.py:30
  178.5 9.3 %collective-permute-start.25 = (f32[3,1,3,1024]{3,2,1,0:T(4,128)S(1)}, f32[3,1,3,1024]{3,2,1,0:T(4,128)S(1)}, u32[]{:S(2)}, u32[]{:S(2)}) collective-permute-start(f32[3,1,3,1024]{3,2,1,0:T(4,128)S(1)} %get-tuple-element.31), channel_id=1, source_target_pairs={{128,0},{256,128},{384,256},{512,384},{640,512},{0,640},{129,1},{2... | collective-permute-start | bytes 110600 | tf_op jit(solution)/shard_map/ppermute | solution.py:33
  187.9 16.1 %collective-permute-start.27 = (f32[3,5,1,1024]{3,2,1,0:T(1,128)S(1)}, f32[3,5,1,1024]{3,2,1,0:T(1,128)S(1)}, u32[]{:S(2)}, u32[]{:S(2)}) collective-permute-start(f32[3,5,1,1024]{3,2,1,0:T(1,128)S(1)} %get-tuple-element.26), channel_id=1, source_target_pairs={{32,0},{64,32},{96,64},{0,96},{33,1},{65,33},{97,65},{1,97},{34,2}... | collective-permute-start | bytes 184328 | tf_op jit(solution)/shard_map/ppermute | solution.py:33
  192.5 11.5 %collective-permute-start.26 = (f32[3,5,1,1024]{3,2,1,0:T(1,128)S(1)}, f32[3,5,1,1024]{3,2,1,0:T(1,128)S(1)}, u32[]{:S(2)}, u32[]{:S(2)}) collective-permute-start(f32[3,5,1,1024]{3,2,1,0:T(1,128)S(1)} %get-tuple-element.25), channel_id=1, source_target_pairs={{0,32},{32,64},{64,96},{96,0},{1,33},{33,65},{65,97},{97,1},{2,34}... | collective-permute-start | bytes 184328 | tf_op jit(solution)/shard_map/ppermute | solution.py:30
  194.5 18.6 %collective-permute-start.19 = (f32[32,6,6,24]{0,3,2,1:T(8,128)S(1)}, f32[32,6,6,24]{0,3,2,1:T(8,128)S(1)}, u32[]{:S(2)}, u32[]{:S(2)}) collective-permute-start(f32[32,6,6,24]{0,3,2,1:T(8,128)S(1)} %get-tuple-element.14), channel_id=1, source_target_pairs={{128,0},{256,128},{384,256},{512,384},{640,512},{0,640},{129,1},{2... | collective-permute-start | bytes 331784 | tf_op jit(solution)/shard_map/ppermute | solution.py:33
  196.5 22.1 %collective-permute-start.18 = (f32[32,6,6,24]{0,3,2,1:T(8,128)S(1)}, f32[32,6,6,24]{0,3,2,1:T(8,128)S(1)}, u32[]{:S(2)}, u32[]{:S(2)}) collective-permute-start(f32[32,6,6,24]{0,3,2,1:T(8,128)S(1)} %get-tuple-element.13), channel_id=1, source_target_pairs={{0,128},{128,256},{256,384},{384,512},{512,640},{640,0},{1,129},{1... | collective-permute-start | bytes 331784 | tf_op jit(solution)/shard_map/ppermute | solution.py:30
  204.2 16.2 %collective-permute-start.29 = (f32[1,5,5,1024]{3,2,1,0:T(8,128)S(1)}, f32[1,5,5,1024]{3,2,1,0:T(8,128)S(1)}, u32[]{:S(2)}, u32[]{:S(2)}) collective-permute-start(f32[1,5,5,1024]{3,2,1,0:T(8,128)S(1)} %get-tuple-element.20), channel_id=1, source_target_pairs={{1,0},{2,1},{3,2},{4,3},{5,4},{6,5},{7,6},{8,7},{9,8},{10,9},{11,1... | collective-permute-start | bytes 307208 | tf_op jit(solution)/shard_map/ppermute | solution.py:33
  206.1 14.3 %collective-permute-start.28 = (f32[1,5,5,1024]{3,2,1,0:T(8,128)S(1)}, f32[1,5,5,1024]{3,2,1,0:T(8,128)S(1)}, u32[]{:S(2)}, u32[]{:S(2)}) collective-permute-start(f32[1,5,5,1024]{3,2,1,0:T(8,128)S(1)} %get-tuple-element.19), channel_id=1, source_target_pairs={{0,1},{1,2},{2,3},{3,4},{4,5},{5,6},{6,7},{7,8},{8,9},{9,10},{10,1... | collective-permute-start | bytes 307208 | tf_op jit(solution)/shard_map/ppermute | solution.py:30
  227.6 12.3 %collective-permute-start.31 = (f32[1,1,1,1024]{3,2,1,0:T(1,128)S(1)}, f32[1,1,1,1024]{3,2,1,0:T(1,128)S(1)}, u32[]{:S(2)}, u32[]{:S(2)}) collective-permute-start(f32[1,1,1,1024]{3,2,1,0:T(1,128)S(1)} %mul.112), channel_id=1, source_target_pairs={{128,0},{256,128},{384,256},{512,384},{640,512},{0,640},{129,1},{2... | collective-permute-start | bytes 12296 | tf_op jit(solution)/shard_map/ppermute | solution.py:33
  239.8 13.1 %collective-permute-start.33 = (f32[1,3,1,1024]{3,2,1,0:T(1,128)S(1)}, f32[1,3,1,1024]{3,2,1,0:T(1,128)S(1)}, u32[]{:S(2)}, u32[]{:S(2)}) collective-permute-start(f32[1,3,1,1024]{3,2,1,0:T(1,128)S(1)} %pad_maximum_fusion.44), channel_id=1, source_target_pairs={{32,0},{64,32},{96,64},{0,96},{33,1},{65,33},{97,65},{1,97},{34,2}... | collective-permute-start | bytes 36872 | tf_op jit(solution)/shard_map/ppermute | solution.py:33
  246.4 16.3 %collective-permute-start.21 = (f32[32,6,20,6]{0,3,2,1:T(8,128)S(1)}, f32[32,6,20,6]{0,3,2,1:T(8,128)S(1)}, u32[]{:S(2)}, u32[]{:S(2)}) collective-permute-start(f32[32,6,20,6]{0,3,2,1:T(8,128)S(1)} %get-tuple-element.10), channel_id=1, source_target_pairs={{32,0},{64,32},{96,64},{0,96},{33,1},{65,33},{97,65},{1,97},{34,2}... | collective-permute-start | bytes 276488 | tf_op jit(solution)/shard_map/ppermute | solution.py:33
  251.0 12.2 %collective-permute-start.20 = (f32[32,6,20,6]{0,3,2,1:T(8,128)S(1)}, f32[32,6,20,6]{0,3,2,1:T(8,128)S(1)}, u32[]{:S(2)}, u32[]{:S(2)}) collective-permute-start(f32[32,6,20,6]{0,3,2,1:T(8,128)S(1)} %get-tuple-element.9), channel_id=1, source_target_pairs={{0,32},{32,64},{64,96},{96,0},{1,33},{33,65},{65,97},{97,1},{2,34}... | collective-permute-start | bytes 276488 | tf_op jit(solution)/shard_map/ppermute | solution.py:30
  253.0 25.1 %collective-permute-start.35 = (f32[1,3,3,1024]{3,2,1,0:T(4,128)S(1)}, f32[1,3,3,1024]{3,2,1,0:T(4,128)S(1)}, u32[]{:S(2)}, u32[]{:S(2)}) collective-permute-start(f32[1,3,3,1024]{3,2,1,0:T(4,128)S(1)} %pad_maximum_fusion.41), channel_id=1, source_target_pairs={{1,0},{2,1},{3,2},{4,3},{5,4},{6,5},{7,6},{8,7},{9,8},{10,9},{11,1... | collective-permute-start | bytes 110600 | tf_op jit(solution)/shard_map/ppermute | solution.py:33
  260.8 17.4 %collective-permute-start.34 = (f32[1,3,3,1024]{3,2,1,0:T(4,128)S(1)}, f32[1,3,3,1024]{3,2,1,0:T(4,128)S(1)}, u32[]{:S(2)}, u32[]{:S(2)}) collective-permute-start(f32[1,3,3,1024]{3,2,1,0:T(4,128)S(1)} %pad_maximum_fusion.41), channel_id=1, source_target_pairs={{0,1},{1,2},{2,3},{3,4},{4,5},{5,6},{6,7},{7,8},{8,9},{9,10},{10,1... | collective-permute-start | bytes 110600 | tf_op jit(solution)/shard_map/ppermute | solution.py:30
  268.3 45.6 %collective-permute-start.23 = (f32[32,6,20,36]{3,0,2,1:T(8,128)}, f32[32,6,20,36]{3,0,2,1:T(8,128)}, u32[]{:S(2)}, u32[]{:S(2)}) collective-permute-start(f32[32,6,20,36]{3,0,2,1:T(8,128)} %copy.136), channel_id=1, source_target_pairs={{1,0},{2,1},{3,2},{4,3},{5,4},{6,5},{7,6},{8,7},{9,8},{10,9},{11,1... | collective-permute-start | bytes 1658888 | tf_op jit(solution)/shard_map/ppermute | solution.py:33
  276.0 45.6 %collective-permute-start.22 = (f32[32,6,20,36]{3,0,2,1:T(8,128)}, f32[32,6,20,36]{3,0,2,1:T(8,128)}, u32[]{:S(2)}, u32[]{:S(2)}) collective-permute-start(f32[32,6,20,36]{3,0,2,1:T(8,128)} %copy.136), channel_id=1, source_target_pairs={{0,1},{1,2},{2,3},{3,4},{4,5},{5,6},{6,7},{7,8},{8,9},{9,10},{10,1... | collective-permute-start | bytes 1658888 | tf_op jit(solution)/shard_map/ppermute | solution.py:30
  331.8 13.5 %collective-permute-start.42 = (f32[3,1,3,1024]{3,2,1,0:T(4,128)S(1)}, f32[3,1,3,1024]{3,2,1,0:T(4,128)S(1)}, u32[]{:S(2)}, u32[]{:S(2)}) collective-permute-start(f32[3,1,3,1024]{3,2,1,0:T(4,128)S(1)} %get-tuple-element.30), channel_id=1, source_target_pairs={{0,128},{128,256},{256,384},{384,512},{512,640},{640,0},{1,129},{1... | collective-permute-start | bytes 110600 | tf_op jit(solution)/shard_map/ppermute | solution.py:30
  343.4 9.3 %collective-permute-start.43 = (f32[3,1,3,1024]{3,2,1,0:T(4,128)S(1)}, f32[3,1,3,1024]{3,2,1,0:T(4,128)S(1)}, u32[]{:S(2)}, u32[]{:S(2)}) collective-permute-start(f32[3,1,3,1024]{3,2,1,0:T(4,128)S(1)} %get-tuple-element.29), channel_id=1, source_target_pairs={{128,0},{256,128},{384,256},{512,384},{640,512},{0,640},{129,1},{2... | collective-permute-start | bytes 110600 | tf_op jit(solution)/shard_map/ppermute | solution.py:33
  352.8 14.9 %collective-permute-start.45 = (f32[3,5,1,1024]{3,2,1,0:T(1,128)S(1)}, f32[3,5,1,1024]{3,2,1,0:T(1,128)S(1)}, u32[]{:S(2)}, u32[]{:S(2)}) collective-permute-start(f32[3,5,1,1024]{3,2,1,0:T(1,128)S(1)} %get-tuple-element.24), channel_id=1, source_target_pairs={{32,0},{64,32},{96,64},{0,96},{33,1},{65,33},{97,65},{1,97},{34,2}... | collective-permute-start | bytes 184328 | tf_op jit(solution)/shard_map/ppermute | solution.py:33
  355.3 12.4 %collective-permute-start.44 = (f32[3,5,1,1024]{3,2,1,0:T(1,128)S(1)}, f32[3,5,1,1024]{3,2,1,0:T(1,128)S(1)}, u32[]{:S(2)}, u32[]{:S(2)}) collective-permute-start(f32[3,5,1,1024]{3,2,1,0:T(1,128)S(1)} %get-tuple-element.23), channel_id=1, source_target_pairs={{0,32},{32,64},{64,96},{96,0},{1,33},{33,65},{65,97},{97,1},{2,34}... | collective-permute-start | bytes 184328 | tf_op jit(solution)/shard_map/ppermute | solution.py:30
  358.2 17.3 %collective-permute-start.37 = (f32[32,6,6,24]{0,3,2,1:T(8,128)S(1)}, f32[32,6,6,24]{0,3,2,1:T(8,128)S(1)}, u32[]{:S(2)}, u32[]{:S(2)}) collective-permute-start(f32[32,6,6,24]{0,3,2,1:T(8,128)S(1)} %get-tuple-element.12), channel_id=1, source_target_pairs={{128,0},{256,128},{384,256},{512,384},{640,512},{0,640},{129,1},{2... | collective-permute-start | bytes 331784 | tf_op jit(solution)/shard_map/ppermute | solution.py:33
  360.1 21.8 %collective-permute-start.36 = (f32[32,6,6,24]{0,3,2,1:T(8,128)S(1)}, f32[32,6,6,24]{0,3,2,1:T(8,128)S(1)}, u32[]{:S(2)}, u32[]{:S(2)}) collective-permute-start(f32[32,6,6,24]{0,3,2,1:T(8,128)S(1)} %get-tuple-element.11), channel_id=1, source_target_pairs={{0,128},{128,256},{256,384},{384,512},{512,640},{640,0},{1,129},{1... | collective-permute-start | bytes 331784 | tf_op jit(solution)/shard_map/ppermute | solution.py:30
  367.8 15.9 %collective-permute-start.47 = (f32[1,5,5,1024]{3,2,1,0:T(8,128)S(1)}, f32[1,5,5,1024]{3,2,1,0:T(8,128)S(1)}, u32[]{:S(2)}, u32[]{:S(2)}) collective-permute-start(f32[1,5,5,1024]{3,2,1,0:T(8,128)S(1)} %get-tuple-element.18), channel_id=1, source_target_pairs={{1,0},{2,1},{3,2},{4,3},{5,4},{6,5},{7,6},{8,7},{9,8},{10,9},{11,1... | collective-permute-start | bytes 307208 | tf_op jit(solution)/shard_map/ppermute | solution.py:33
  371.2 14.7 %collective-permute-start.46 = (f32[1,5,5,1024]{3,2,1,0:T(8,128)S(1)}, f32[1,5,5,1024]{3,2,1,0:T(8,128)S(1)}, u32[]{:S(2)}, u32[]{:S(2)}) collective-permute-start(f32[1,5,5,1024]{3,2,1,0:T(8,128)S(1)} %get-tuple-element.17), channel_id=1, source_target_pairs={{0,1},{1,2},{2,3},{3,4},{4,5},{5,6},{6,7},{7,8},{8,9},{9,10},{10,1... | collective-permute-start | bytes 307208 | tf_op jit(solution)/shard_map/ppermute | solution.py:30
  391.2 11.5 %collective-permute-start.49 = (f32[1,1,1,1024]{3,2,1,0:T(1,128)S(1)}, f32[1,1,1,1024]{3,2,1,0:T(1,128)S(1)}, u32[]{:S(2)}, u32[]{:S(2)}) collective-permute-start(f32[1,1,1,1024]{3,2,1,0:T(1,128)S(1)} %mul.119), channel_id=1, source_target_pairs={{128,0},{256,128},{384,256},{512,384},{640,512},{0,640},{129,1},{2... | collective-permute-start | bytes 12296 | tf_op jit(solution)/shard_map/ppermute | solution.py:33
  393.5 9.2 %collective-permute-start.48 = (f32[1,1,1,1024]{3,2,1,0:T(1,128)S(1)}, f32[1,1,1,1024]{3,2,1,0:T(1,128)S(1)}, u32[]{:S(2)}, u32[]{:S(2)}) collective-permute-start(f32[1,1,1,1024]{3,2,1,0:T(1,128)S(1)} %mul.119), channel_id=1, source_target_pairs={{0,128},{128,256},{256,384},{384,512},{512,640},{640,0},{1,129},{1... | collective-permute-start | bytes 12296 | tf_op jit(solution)/shard_map/ppermute | solution.py:30
  402.7 11.6 %collective-permute-start.51 = (f32[1,3,1,1024]{3,2,1,0:T(1,128)S(1)}, f32[1,3,1,1024]{3,2,1,0:T(1,128)S(1)}, u32[]{:S(2)}, u32[]{:S(2)}) collective-permute-start(f32[1,3,1,1024]{3,2,1,0:T(1,128)S(1)} %pad_maximum_fusion.45), channel_id=1, source_target_pairs={{32,0},{64,32},{96,64},{0,96},{33,1},{65,33},{97,65},{1,97},{34,2}... | collective-permute-start | bytes 36872 | tf_op jit(solution)/shard_map/ppermute | solution.py:33
  408.1 13.9 %collective-permute-start.39 = (f32[32,6,20,6]{0,3,2,1:T(8,128)S(1)}, f32[32,6,20,6]{0,3,2,1:T(8,128)S(1)}, u32[]{:S(2)}, u32[]{:S(2)}) collective-permute-start(f32[32,6,20,6]{0,3,2,1:T(8,128)S(1)} %get-tuple-element.8), channel_id=1, source_target_pairs={{32,0},{64,32},{96,64},{0,96},{33,1},{65,33},{97,65},{1,97},{34,2}... | collective-permute-start | bytes 276488 | tf_op jit(solution)/shard_map/ppermute | solution.py:33
  412.4 12.3 %collective-permute-start.38 = (f32[32,6,20,6]{0,3,2,1:T(8,128)S(1)}, f32[32,6,20,6]{0,3,2,1:T(8,128)S(1)}, u32[]{:S(2)}, u32[]{:S(2)}) collective-permute-start(f32[32,6,20,6]{0,3,2,1:T(8,128)S(1)} %get-tuple-element.7), channel_id=1, source_target_pairs={{0,32},{32,64},{64,96},{96,0},{1,33},{33,65},{65,97},{97,1},{2,34}... | collective-permute-start | bytes 276488 | tf_op jit(solution)/shard_map/ppermute | solution.py:30
  414.4 23.9 %collective-permute-start.53 = (f32[1,3,3,1024]{3,2,1,0:T(4,128)S(1)}, f32[1,3,3,1024]{3,2,1,0:T(4,128)S(1)}, u32[]{:S(2)}, u32[]{:S(2)}) collective-permute-start(f32[1,3,3,1024]{3,2,1,0:T(4,128)S(1)} %pad_maximum_fusion.42), channel_id=1, source_target_pairs={{1,0},{2,1},{3,2},{4,3},{5,4},{6,5},{7,6},{8,7},{9,8},{10,9},{11,1... | collective-permute-start | bytes 110600 | tf_op jit(solution)/shard_map/ppermute | solution.py:33
  420.1 18.2 %collective-permute-start.52 = (f32[1,3,3,1024]{3,2,1,0:T(4,128)S(1)}, f32[1,3,3,1024]{3,2,1,0:T(4,128)S(1)}, u32[]{:S(2)}, u32[]{:S(2)}) collective-permute-start(f32[1,3,3,1024]{3,2,1,0:T(4,128)S(1)} %pad_maximum_fusion.42), channel_id=1, source_target_pairs={{0,1},{1,2},{2,3},{3,4},{4,5},{5,6},{6,7},{7,8},{8,9},{9,10},{10,1... | collective-permute-start | bytes 110600 | tf_op jit(solution)/shard_map/ppermute | solution.py:30
  429.7 44.9 %collective-permute-start.41 = (f32[32,6,20,36]{3,0,2,1:T(8,128)}, f32[32,6,20,36]{3,0,2,1:T(8,128)}, u32[]{:S(2)}, u32[]{:S(2)}) collective-permute-start(f32[32,6,20,36]{3,0,2,1:T(8,128)} %copy.148), channel_id=1, source_target_pairs={{1,0},{2,1},{3,2},{4,3},{5,4},{6,5},{7,6},{8,7},{9,8},{10,9},{11,1... | collective-permute-start | bytes 1658888 | tf_op jit(solution)/shard_map/ppermute | solution.py:33
  436.0 46.3 %collective-permute-start.40 = (f32[32,6,20,36]{3,0,2,1:T(8,128)}, f32[32,6,20,36]{3,0,2,1:T(8,128)}, u32[]{:S(2)}, u32[]{:S(2)}) collective-permute-start(f32[32,6,20,36]{3,0,2,1:T(8,128)} %copy.148), channel_id=1, source_target_pairs={{0,1},{1,2},{2,3},{3,4},{4,5},{5,6},{6,7},{7,8},{8,9},{9,10},{10,1... | collective-permute-start | bytes 1658888 | tf_op jit(solution)/shard_map/ppermute | solution.py:30
  (48 other events, 1055.0 us)
where the time goes:
time: 497 us; the launch traced here: 492 us
  starting transfers between devices  224 us (45%)
  waiting for transfers between devices  162 us (33%)
  local copies, waits for them, and re-layouts  56.5 us (11%)
  matrix products  31.8 us (6%)
  other arithmetic  15.8 us (3%)
    ppermute x27, waiting for transfers between devices, with_halo(): lax.ppermute(lax.slice_in_dim(block, 0, width, axis=dim), axis, backward)  122 us
    ppermute x27, starting transfers between devices, with_halo(): lax.ppermute(lax.slice_in_dim(block, 0, width, axis=dim), axis, backward)  116 us
    ppermute x27, starting transfers between devices, with_halo(): lax.ppermute(lax.slice_in_dim(block, block.shape[dim] - width, None, axis...  108 us
    ppermute x27, waiting for transfers between devices, with_halo(): lax.ppermute(lax.slice_in_dim(block, block.shape[dim] - width, None, axis...  40.1 us
    slice x3, local copies, waits for them, and re-layouts, nonlocal_term(): summed = jnp.sum(padded[0::2, 0::2, 0::2], axis=(0, 1, 2))  14.5 us
    concatenate x19, other arithmetic, with_halo(): block = jnp.concatenate([low, block, high], axis=dim)  12.9 us
    concatenate x7, local copies, waits for them, and re-layouts, with_halo(): block = jnp.concatenate([low, block, high], axis=dim)  11.1 us
    ppermute x3, local copies, waits for them, and re-layouts, with_halo(): lax.ppermute(lax.slice_in_dim(block, block.shape[dim] - width, None, axis...  10.3 us
  transfers between devices with their start and end apart: 54, of which 19 were waited for; matrix products, arithmetic and copies ran while one was open for 12% of the time, Pallas kernels for 0%

commit v1 on v0

v1 whole, which is shorter than its diff:
```python
import functools

import jax
import jax.numpy as jnp
from jax import lax
from jax.experimental import pallas as pl
from jax.experimental.pallas import tpu as pltpu
from jax.sharding import PartitionSpec as P

MESH = pl.DeviceIdType.MESH
F32, BF16 = jnp.float32, jnp.bfloat16

DEGREE = 3
NORB, NPJ, SLOTS, ATOM_DEV = 32, 4, 16, 8
CZ, CX, CY = 6, 8, 24
PROWS = SLOTS * NPJ
ZI, XI = CZ // 2, CX // 2
ROWS = ZI * XI * CY
SEG_CELLS = XI * CY

STENCIL = (
    -5369.0 / 1800.0,
    12.0 / 7.0,
    -15.0 / 56.0,
    10.0 / 189.0,
    -1.0 / 112.0,
    2.0 / 1925.0,
    -1.0 / 16632.0,
)
LOWER_EDGE = 2.0
UPPER_EDGE = 16.0
CENTRE = 0.5 * (UPPER_EDGE + LOWER_EDGE)
SPREAD = 0.5 * (UPPER_EDGE - LOWER_EDGE)
WEIGHT = tuple(-0.5 * c / SPREAD for c in STENCIL)

OFFSETS = [
    (a - 1, b - 1, c - 1)
    for a in range(3)
    for b in range(3)
    for c in range(3)
    if (a, b, c) != (1, 1, 1)
]
BESIDE = len(OFFSETS)


def split2(value):
    high = value.astype(BF16)
    low = (value - high.astype(F32)).astype(BF16)
    return high, low


def split3(value):
    high = value.astype(BF16)
    rest = value - high.astype(F32)
    mid = rest.astype(BF16)
    low = (rest - mid.astype(F32)).astype(BF16)
    return high, mid, low


def dot(a, b):
    return jnp.dot(a, b, preferred_element_type=F32)


def lanes_of(shape):
    return lax.broadcasted_iota(jnp.int32, shape, len(shape) - 1)


def roll(value, shift):
    return pltpu.roll(value, shift, value.ndim - 1)


def kernel(
    sizes,
    orb_hbm,
    pot_ref,
    proj_hbm,
    targets_ref,
    coupling_ref,
    out_ref,
    orb,
    proj,
    field,
    z_low,
    z_high,
    x_low,
    x_high,
    x_low_part,
    x_high_part,
    send_low_part,
    send_high_part,
    grouped,
    partials,
    scaled,
    gathered,
    rows_t,
    rows_hi,
    rows_lo,
    columns,
    choose,
    pick,
    factor,
    diagonal,
    pot_pad,
    local,
    in_sems,
    halo_send,
    halo_recv,
    sum_send,
    sum_recv,
    spread_send,
    spread_recv,
):
    me = {name: lax.axis_index(name) for name in ("gz", "gx", "gy")}

    def beside(offset):
        place = {
            name: lax.rem(me[name] + step + sizes[name], sizes[name])
            for name, step in zip(("gz", "gx", "gy"), offset)
        }
        return (place["gx"], place["gy"], place["gz"])

    targets = [beside(offset) for offset in OFFSETS]

    load_orb = pltpu.make_async_copy(orb_hbm, orb, in_sems.at[0])
    load_proj = pltpu.make_async_copy(proj_hbm, proj, in_sems.at[1])
    load_orb.start()
    load_proj.start()

    barrier = pltpu.get_barrier_semaphore()
    for place in targets:
        pl.semaphore_signal(barrier, inc=1, device_id=place, device_id_type=MESH)

    load_orb.wait()
    for zi in range(ZI):
        for xi in range(XI):
            for q in range(4):
                zb, xb = q // 2, q % 2
                field[0, zi, xi, 8:32, 32 * q : 32 * q + 32] = orb[zb * ZI + zi, xb * XI + xi]

    load_proj.wait()
    for q in range(4):
        zb, xb = q // 2, q % 2
        for zi in range(ZI):
            start = (zb * ZI + zi) * CX * CY + xb * SEG_CELLS
            rows_t[PROWS * q : PROWS * (q + 1), SEG_CELLS * zi : SEG_CELLS * (zi + 1)] = proj[
                :, start : start + SEG_CELLS
            ]
    rows_t[:, ROWS:384] = jnp.zeros((4 * PROWS, 384 - ROWS), F32)
    high, low = split2(rows_t[...])
    rows_hi[...] = high
    rows_lo[...] = low

    lane_slot = lanes_of((8, 256)) % PROWS // NPJ
    row_slot = lax.broadcasted_iota(jnp.int32, (PROWS, 256), 0) // NPJ
    named_lane = jnp.zeros((8, 256), jnp.int32)
    named_row = jnp.zeros((PROWS, 256), jnp.int32)
    own_first = ATOM_DEV * (BESIDE // 2)
    for s in range(SLOTS):
        atom = targets_ref[s]
        atom = jnp.where(
            atom < own_first,
            atom,
            jnp.where(atom < own_first + ATOM_DEV, atom + own_first, atom - ATOM_DEV),
        )
        named_lane = jnp.where(lane_slot == s, atom, named_lane)
        named_row = jnp.where(row_slot == s, atom, named_row)
    atom_row = lax.broadcasted_iota(jnp.int32, (8, 256), 0)
    used = lanes_of((8, 256)) < 3 * PROWS
    for j in range(BESIDE + 1):
        choose[8 * j : 8 * j + 8, :] = jnp.where(
            (named_lane == atom_row + 8 * j) & used, 1.0, 0.0
        )
    pick[...] = jnp.where(named_row == lanes_of((PROWS, 256)), 1.0, 0.0)
    pair = NPJ * lax.broadcasted_iota(jnp.int32, (8, 128), 0) + lanes_of((8, 128)) // NORB
    weights = jnp.zeros((8, 128), F32)
    for j in range(ATOM_DEV * NPJ):
        weights = jnp.where(pair == j, coupling_ref[j], weights)
    factor[...] = weights * (1.0 / SPREAD)

    group = lanes_of((PROWS, 128)) // NORB
    own_group = group == lax.broadcasted_iota(jnp.int32, (PROWS, 128), 0) % NPJ
    is_x1 = lanes_of((CY, 128)) % 64 >= 32
    is_z1 = lanes_of((CY, 128)) >= 64

    pl.semaphore_wait(barrier, BESIDE)

    def everywhere(masked):
        paired = masked + roll(masked, 64)
        return paired + roll(paired, 32)

    def send_sums(k):
        flat = field[k, :, :, 8:32, :].reshape(ROWS, 128)
        f_hi, f_lo = split2(flat)
        p_hi, p_lo = rows_hi[:, :ROWS], rows_lo[:, :ROWS]
        crossed = dot(p_hi, f_hi) + (dot(p_lo, f_hi) + dot(p_hi, f_lo))
        kept = crossed[3 * PROWS :]
        for q in range(3):
            kept = jnp.where(group == q, crossed[PROWS * q : PROWS * (q + 1)], kept)
        by_slot = jnp.where(own_group, everywhere(kept), 0.0)
        parts = split3(by_slot)
        stacked = jnp.concatenate(parts + (jnp.zeros((PROWS, 128), BF16),), axis=0)
        sums = dot(choose[...].astype(BF16), stacked)
        grouped[k] = sums.reshape(BESIDE + 1, 8, 128)
        copies = []
        for j, place in enumerate(targets):
            copies.append(
                pltpu.make_async_remote_copy(
                    src_ref=grouped.at[k, j],
                    dst_ref=partials.at[k, j],
                    send_sem=sum_send.at[k],
                    recv_sem=sum_recv.at[k],
                    device_id=place,
                    device_id_type=MESH,
                )
            )
            copies[-1].start()

    def halo_copies(k):
        own = field.at[k, :, :, pl.ds(8, CY), :]
        moves = (
            (field.at[k, :, pl.ds(2, 2), pl.ds(8, CY), :], x_low.at[k], (0, 1, 0)),
            (field.at[k, :, pl.ds(0, 2), pl.ds(8, CY), :], x_high.at[k], (0, -1, 0)),
            (send_low_part.at[k], x_low_part.at[k], (0, 1, 0)),
            (send_high_part.at[k], x_high_part.at[k], (0, -1, 0)),
            (own, z_low.at[k], (1, 0, 0)),
            (own, z_high.at[k], (-1, 0, 0)),
            (field.at[k, :, :, pl.ds(24, 8), :], field.at[k, :, :, pl.ds(0, 8), :], (0, 0, 1)),
            (field.at[k, :, :, pl.ds(8, 8), :], field.at[k, :, :, pl.ds(32, 8), :], (0, 0, -1)),
        )
        return [
            pltpu.make_async_remote_copy(
                src_ref=source,
                dst_ref=target,
                send_sem=halo_send.at[k, i],
                recv_sem=halo_recv.at[k, i],
                device_id=beside(offset),
                device_id_type=MESH,
            )
            for i, (source, target, offset) in enumerate(moves)
        ]

    def send_halos(k):
        for zi in range(ZI):
            cell = [field[k, zi, xi, 8:32, :] for xi in range(XI)]
            send_low_part[k, zi] = jnp.where(is_x1, cell[1], roll(cell[0], 96))
            send_high_part[k, zi] = jnp.where(is_x1, roll(cell[2], 32), cell[3])
        copies = halo_copies(k)
        for copy in copies:
            copy.start()
        return copies

    pot_pad[...] = jnp.zeros((128, 128), F32)
    pot_pad[: CZ * CX, :CY] = pot_ref[...]
    pot_t = pot_pad[...].T[:CY]
    pieces = split3(pot_t)
    stacked_pot = jnp.concatenate([p.astype(F32) for p in pieces], axis=0).astype(BF16)
    plane = lax.broadcasted_iota(jnp.int32, (128, 128), 0)
    lane = lanes_of((128, 128))
    wanted = (lane // 64 * ZI) * CX + lane // 32 % 2 * XI

    def fill_diagonal():
        for zi in range(ZI):
            for xi in range(XI):
                hot = jnp.where(plane == wanted + (zi * CX + xi), 1.0, 0.0).astype(BF16)
                got = dot(stacked_pot, hot)
                value = got[:CY] + (got[CY : 2 * CY] + got[2 * CY :])
                diagonal[zi, xi] = (value - (CENTRE + 1.5 * STENCIL[0])) * (1.0 / SPREAD)

    def fill_columns():
        transposed = rows_t[...].T[:ROWS]
        t_hi, t_lo = split2(transposed)
        columns[:, 0:256] = t_hi
        columns[:, 256:512] = t_lo
        columns[:, 512:768] = t_hi

    def send_atoms(k):
        pltpu.make_async_copy(partials.at[k], partials.at[k], sum_recv.at[k]).wait()
        total = grouped[k, BESIDE]
        for j in range(BESIDE):
            total = total + partials[k, j]
        total = total * factor[...]
        scaled[k] = total
        gathered[k, BESIDE] = total
        for j in range(BESIDE + 1, 32):
            gathered[k, j] = jnp.zeros((8, 128), F32)
        for j, place in enumerate(targets):
            pltpu.make_async_remote_copy(
                src_ref=scaled.at[k],
                dst_ref=gathered.at[k, BESIDE - 1 - j],
                send_sem=spread_send.at[k],
                recv_sem=spread_recv.at[k],
                device_id=place,
                device_id_type=MESH,
            ).start()

    def stencil(k, copies):
        for copy in copies:
            copy.wait_recv()
        for xi in range(XI):
            own = [field[k, zi, xi, 8:32, :] for zi in range(ZI)]
            low = [z_low[k, zi, xi] for zi in range(ZI)]
            high = [z_high[k, zi, xi] for zi in range(ZI)]
            before = [roll(jnp.where(is_z1, l, o), 64) for o, l in zip(own, low)]
            after = [roll(jnp.where(is_z1, o, h), 64) for o, h in zip(own, high)]
            line = low + before + own + after + high
            for zi in range(ZI):
                at = zi + 2 * ZI
                total = diagonal[zi, xi] * own[zi]
                for d in range(1, 7):
                    total = total + WEIGHT[d] * (line[at - d] + line[at + d])
                for d in range(1, 7):
                    total = total + WEIGHT[d] * (
                        field[k, zi, xi, 8 - d : 32 - d, :] + field[k, zi, xi, 8 + d : 32 + d, :]
                    )
                local[zi, xi] = total
        for zi in range(ZI):
            own = [field[k, zi, xi, 8:32, :] for xi in range(XI)]
            up = [roll(o, 32) for o in own]
            down = [roll(o, 96) for o in own]
            low = [x_low[k, zi, i] for i in range(2)]
            high = [x_high[k, zi, i] for i in range(2)]
            low_part, high_part = x_low_part[k, zi], x_high_part[k, zi]
            before = [
                jnp.where(is_x1, up[0], low_part),
                jnp.where(is_x1, up[1], roll(low_part, 96)),
                jnp.where(is_x1, up[2], roll(low[0], 96)),
                jnp.where(is_x1, up[3], roll(low[1], 96)),
            ]
            after = [
                jnp.where(is_x1, roll(high[0], 32), down[0]),
                jnp.where(is_x1, roll(high[1], 32), down[1]),
                jnp.where(is_x1, high_part, down[2]),
                jnp.where(is_x1, roll(high_part, 32), down[3]),
            ]
            line = low + before + own + after + high
            for xi in range(XI):
                at = xi + 6
                total = local[zi, xi]
                for d in range(1, 7):
                    total = total + WEIGHT[d] * (line[at - d] + line[at + d])
                local[zi, xi] = total

    def nonlocal_part(k):
        landed = gathered.at[k, pl.ds(0, BESIDE)]
        pltpu.make_async_copy(landed, landed, spread_recv.at[k]).wait()
        around = gathered[k].reshape(256, 128)
        hot = pick[...].astype(BF16)
        a, b, c = split3(around)
        picked = dot(hot, a) + (dot(hot, b) + dot(hot, c))
        rep = everywhere(jnp.where(own_group, picked, 0.0))
        blocks = jnp.concatenate([jnp.where(group == q, rep, 0.0) for q in range(4)], axis=0)
        b_hi, b_lo = split2(blocks)
        return dot(columns[...], jnp.concatenate([b_hi, b_hi, b_lo], axis=0))

    started = []
    for k in range(DEGREE):
        send_sums(k)
        copies = send_halos(k)
        started += copies
        if k == 0:
            fill_diagonal()
            fill_columns()
        send_atoms(k)
        stencil(k, copies)
        returned = nonlocal_part(k).reshape(ZI, XI, CY, 128)
        for zi in range(ZI):
            for xi in range(XI):
                value = local[zi, xi] + returned[zi, xi]
                if k > 0:
                    value = 2.0 * value - field[k - 1, zi, xi, 8:32, :]
                if k < DEGREE - 1:
                    field[k + 1, zi, xi, 8:32, :] = value
                else:
                    for q in range(4):
                        zb, xb = q // 2, q % 2
                        out_ref[zb * ZI + zi, xb * XI + xi] = value[:, 32 * q : 32 * q + 32]

    for copy in started:
        copy.wait_send()
    for k in range(DEGREE):
        sent = grouped.at[k, pl.ds(0, BESIDE)]
        pltpu.make_async_copy(sent, sent, sum_send.at[k]).wait()
        pltpu.make_async_copy(sent, sent, spread_send.at[k]).wait()


def shards(sizes, orbitals, potential, projectors, targets, coupling):
    cells = orbitals.transpose(1, 2, 3, 0)
    any_space = pl.BlockSpec(memory_space=pl.ANY)
    vmem = pl.BlockSpec(memory_space=pltpu.VMEM)
    smem = pl.BlockSpec(memory_space=pltpu.SMEM)
    steps = DEGREE
    result = pl.pallas_call(
        functools.partial(kernel, sizes),
        out_shape=jax.ShapeDtypeStruct((CZ, CX, CY, NORB), F32),
        in_specs=[any_space, vmem, any_space, smem, smem],
        out_specs=vmem,
        scratch_shapes=[
            pltpu.VMEM((CZ, CX, CY, NORB), F32),
            pltpu.VMEM((PROWS, CZ * CX * CY), F32),
            pltpu.VMEM((steps, ZI, XI, CY + 16, 128), F32),
            pltpu.VMEM((steps, ZI, XI, CY, 128), F32),
            pltpu.VMEM((steps, ZI, XI, CY, 128), F32),
            pltpu.VMEM((steps, ZI, 2, CY, 128), F32),
            pltpu.VMEM((steps, ZI, 2, CY, 128), F32),
            pltpu.VMEM((steps, ZI, CY, 128), F32),
            pltpu.VMEM((steps, ZI, CY, 128), F32),
            pltpu.VMEM((steps, ZI, CY, 128), F32),
            pltpu.VMEM((steps, ZI, CY, 128), F32),
            pltpu.VMEM((steps, BESIDE + 1, 8, 128), F32),
            pltpu.VMEM((steps, BESIDE, 8, 128), F32),
            pltpu.VMEM((steps, 8, 128), F32),
            pltpu.VMEM((steps, 32, 8, 128), F32),
            pltpu.VMEM((4 * PROWS, 384), F32),
            pltpu.VMEM((4 * PROWS, 384), BF16),
            pltpu.VMEM((4 * PROWS, 384), BF16),
            pltpu.VMEM((ROWS, 768), BF16),
            pltpu.VMEM((8 * (BESIDE + 1), 256), F32),
            pltpu.VMEM((PROWS, 256), F32),
            pltpu.VMEM((8, 128), F32),
            pltpu.VMEM((ZI, XI, CY, 128), F32),
            pltpu.VMEM((128, 128), F32),
            pltpu.VMEM((ZI, XI, CY, 128), F32),
            pltpu.SemaphoreType.DMA((2,)),
            pltpu.SemaphoreType.DMA((steps, 8)),
            pltpu.SemaphoreType.DMA((steps, 8)),
            pltpu.SemaphoreType.DMA((steps,)),
            pltpu.SemaphoreType.DMA((steps,)),
            pltpu.SemaphoreType.DMA((steps,)),
            pltpu.SemaphoreType.DMA((steps,)),
        ],
        compiler_params=pltpu.CompilerParams(
            collective_id=0, has_side_effects=True, vmem_limit_bytes=40 * 1024 * 1024
        ),
    )(
        cells,
        potential.reshape(CZ * CX, CY),
        projectors.reshape(PROWS, CZ * CX * CY),
        targets.reshape(SLOTS),
        coupling.reshape(ATOM_DEV * NPJ),
    )
    return result.transpose(3, 0, 1, 2)


def solution(mesh):
    sizes = {name: mesh.shape[name] for name in ("gx", "gy", "gz")}
    return jax.shard_map(
        functools.partial(shards, sizes),
        mesh=mesh,
        in_specs=(
            P(None, "gz", "gx", "gy"),
            P("gz", "gx", "gy"),
            P("gz", "gx", "gy", None, None),
            P("gz", "gx", "gy", None),
            P("gz", "gx", "gy", None),
        ),
        out_specs=P(None, "gz", "gx", "gy"),
        check_vma=False,
    )
```

time: 497 us -> 79.7 us (0.16); the launches traced: 492 us -> 79.5 us
  starting transfers between devices: 224 us -> 0 us
  waiting for transfers between devices: 162 us -> 0 us
  Pallas kernels: 0 us -> 75.2 us
  local copies, waits for them, and re-layouts: 56.5 us -> 4.25 us
  matrix products: 31.8 us -> 0 us
  other arithmetic: 15.8 us -> 0 us
    ppermute x54 -> x0, starting transfers between devices: 224 us -> none  [the longest x27 116 us: with_halo(): lax.ppermute(lax.slice_in_dim(block, 0, width, axis=dim), axis, backward)]
    ppermute x54 -> x0, waiting for transfers between devices: 162 us -> none  [the longest x27 122 us: with_halo(): lax.ppermute(lax.slice_in_dim(block, 0, width, axis=dim), axis, backward)]
    pallas_call x0 -> x1, Pallas kernels: none -> 75.2 us  [shards(): pl.pallas_call(functools.partial(kernel, sizes), out_shape=jax.ShapeDtype...]
    dot_general x21 -> x0, matrix products: 31.8 us -> none  [the longest x3 7.67 us: stencil_sum(): jnp.einsum('nzxy,zw->nwxy', extended[0], band_table(values_in.shape[1]),...]
    ppermute x6 -> x0, local copies, waits for them, and re-layouts: 20.4 us -> none  [the longest x3 10.3 us: with_halo(): lax.ppermute(lax.slice_in_dim(block, block.shape[dim] - width, None, axis...]
    slice x16 -> x0, local copies, waits for them, and re-layouts: 18.1 us -> none  [the longest x3 14.5 us: nonlocal_term(): summed = jnp.sum(padded[0::2, 0::2, 0::2], axis=(0, 1, 2))]
    concatenate x19 -> x0, other arithmetic: 12.9 us -> none  [with_halo(): block = jnp.concatenate([low, block, high], axis=dim)]
    concatenate x7 -> x0, local copies, waits for them, and re-layouts: 11.1 us -> none  [with_halo(): block = jnp.concatenate([low, block, high], axis=dim)]
  transfers between devices with their start and end apart: 54 -> 0, of which waited for: 19 -> 0; matrix products, arithmetic and copies ran while one was open for 12% -> 0% of each run, Pallas kernels for 0% -> 0%
where the time goes in v1:
time: 79.7 us; the launch traced here: 79.5 us
  Pallas kernels  75.2 us (94%)
  local copies, waits for them, and re-layouts  4.25 us (5%)
    pallas_call x1, Pallas kernels, shards(): pl.pallas_call(functools.partial(kernel, sizes), out_shape=jax.ShapeDtype...  75.2 us
    unnamed x11, local copies, waits for them, and re-layouts  4.25 us

profile of v1, /device:TPU:1, one launch (start us, length us, event | category | flops | bytes accessed | tf_op | source)
XLA Modules:
  0.0 79.5 jit_solution(7062646579912005300)
XLA Ops:
  0.0 0.0 copy-start.3
  0.0 0.0 copy-start.4
  0.0 0.7 copy-done.3
  0.7 0.0 copy-done.4
  0.7 0.0 copy-start
  0.7 1.1 %copy-done = f32[32,6,8,24]{0,3,2,1:T(8,128)S(1)} copy-done((f32[32,6,8,24]{0,3,2,1:T(8,128)S(1)}, f32[32,6,8,24]{0,3,2,1:T(8,128)}, u32[]{:S(2)}) %copy-start) | copy-done | bytes 147480
  1.7 0.0 copy-start.1
  1.7 1.0 %copy-done.1 = f32[1,1,1,64,1152]{4,3,2,1,0:T(8,128)S(1)} copy-done((f32[1,1,1,64,1152]{4,3,2,1,0:T(8,128)S(1)}, f32[1,1,1,64,1152]{4,3,2,1,0:T(8,128)}, u32[]{:S(2)}) %copy-start.1) | copy-done | bytes 294936
  2.7 0.0 copy-start.2
  2.7 0.7 copy-done.2
  3.4 75.2 %shard_map.55 = f32[6,8,24,32]{3,2,1,0:T(8,128)S(1)} custom-call(f32[6,8,24,32]{3,2,1,0:T(8,128)S(1)} %bitcast.7, f32[48,24]{1,0:T(8,128)S(1)} %bitcast.9, f32[64,1152]{1,0:T(8,128)S(1)} %bitcast.8, s32[16]{0:T(128)S(1)} %bitcast.10, f32[32]{0:T(128)S(1)} %bitcast.11), custom_call_target="tpu_custom_call" | custom-call | tf_op jit(solution)/shard_map/pallas_call | solution.py:392
  78.6 0.8 %copy.7 = f32[32,6,8,24]{0,3,2,1:T(8,128)} copy(f32[32,6,8,24]{0,3,2,1:T(8,128)S(1)} %bitcast.6) | data formatting | bytes 294912
Async XLA Ops:
  0.0 0.7 copy-start.3
  0.0 0.7 copy-start.4
  0.7 1.1 %copy-start = (f32[32,6,8,24]{0,3,2,1:T(8,128)S(1)}, f32[32,6,8,24]{0,3,2,1:T(8,128)}, u32[]{:S(2)}) copy-start(f32[32,6,8,24]{0,3,2,1:T(8,128)} %param.5) | copy-start | bytes 442372
  1.7 1.0 %copy-start.1 = (f32[1,1,1,64,1152]{4,3,2,1,0:T(8,128)S(1)}, f32[1,1,1,64,1152]{4,3,2,1,0:T(8,128)}, u32[]{:S(2)}) copy-start(f32[1,1,1,64,1152]{4,3,2,1,0:T(8,128)} %param.7) | copy-start | bytes 884740
  2.7 0.7 copy-start.2

commit v2 on v1

--- a/solution.py
+++ b/solution.py
@@ -72,13 +72,16 @@
 def kernel(
     sizes,
     orb_hbm,
-    pot_ref,
+    pot_hbm,
     proj_hbm,
-    targets_ref,
-    coupling_ref,
+    targets_hbm,
+    coupling_hbm,
     out_ref,
     orb,
     proj,
+    pot_ref,
+    targets_ref,
+    coupling_ref,
     field,
     z_low,
     z_high,
@@ -98,6 +101,7 @@
     columns,
     choose,
     pick,
+    overlap,
     factor,
     diagonal,
     pot_pad,
@@ -121,23 +125,33 @@
 
     targets = [beside(offset) for offset in OFFSETS]
 
-    load_orb = pltpu.make_async_copy(orb_hbm, orb, in_sems.at[0])
-    load_proj = pltpu.make_async_copy(proj_hbm, proj, in_sems.at[1])
-    load_orb.start()
-    load_proj.start()
-
     barrier = pltpu.get_barrier_semaphore()
     for place in targets:
         pl.semaphore_signal(barrier, inc=1, device_id=place, device_id_type=MESH)
 
-    load_orb.wait()
+    loads = [
+        pltpu.make_async_copy(source, target, in_sems.at[i])
+        for i, (source, target) in enumerate(
+            (
+                (orb_hbm, orb),
+                (proj_hbm, proj),
+                (targets_hbm, targets_ref),
+                (coupling_hbm, coupling_ref),
+                (pot_hbm, pot_ref),
+            )
+        )
+    ]
+    for load in loads:
+        load.start()
+
+    loads[0].wait()
     for zi in range(ZI):
         for xi in range(XI):
             for q in range(4):
                 zb, xb = q // 2, q % 2
                 field[0, zi, xi, 8:32, 32 * q : 32 * q + 32] = orb[zb * ZI + zi, xb * XI + xi]
 
-    load_proj.wait()
+    loads[1].wait()
     for q in range(4):
         zb, xb = q // 2, q % 2
         for zi in range(ZI):
@@ -150,9 +164,11 @@
     rows_hi[...] = high
     rows_lo[...] = low
 
-    lane_slot = lanes_of((8, 256)) % PROWS // NPJ
+    loads[2].wait()
+    loads[3].wait()
+    lane_slot = lanes_of((8, 128)) % PROWS // NPJ
     row_slot = lax.broadcasted_iota(jnp.int32, (PROWS, 256), 0) // NPJ
-    named_lane = jnp.zeros((8, 256), jnp.int32)
+    named_lane = jnp.zeros((8, 128), jnp.int32)
     named_row = jnp.zeros((PROWS, 256), jnp.int32)
     own_first = ATOM_DEV * (BESIDE // 2)
     for s in range(SLOTS):
@@ -164,13 +180,13 @@
         )
         named_lane = jnp.where(lane_slot == s, atom, named_lane)
         named_row = jnp.where(row_slot == s, atom, named_row)
-    atom_row = lax.broadcasted_iota(jnp.int32, (8, 256), 0)
-    used = lanes_of((8, 256)) < 3 * PROWS
+    atom_row = lax.broadcasted_iota(jnp.int32, (8, 128), 0)
     for j in range(BESIDE + 1):
-        choose[8 * j : 8 * j + 8, :] = jnp.where(
-            (named_lane == atom_row + 8 * j) & used, 1.0, 0.0
-        )
-    pick[...] = jnp.where(named_row == lanes_of((PROWS, 256)), 1.0, 0.0)
+        choose[8 * j : 8 * j + 8, :] = jnp.where(named_lane == atom_row + 8 * j, 1.0, 0.0)
+    pick[...] = jnp.where(named_row == lanes_of((PROWS, 256)), 1.0, 0.0).astype(BF16)
+    for k in range(DEGREE):
+        for j in range(BESIDE + 1, 32):
+            gathered[k, j] = jnp.zeros((8, 128), F32)
     pair = NPJ * lax.broadcasted_iota(jnp.int32, (8, 128), 0) + lanes_of((8, 128)) // NORB
     weights = jnp.zeros((8, 128), F32)
     for j in range(ATOM_DEV * NPJ):
@@ -182,38 +198,33 @@
     is_x1 = lanes_of((CY, 128)) % 64 >= 32
     is_z1 = lanes_of((CY, 128)) >= 64
 
-    pl.semaphore_wait(barrier, BESIDE)
-
     def everywhere(masked):
         paired = masked + roll(masked, 64)
         return paired + roll(paired, 32)
 
-    def send_sums(k):
-        flat = field[k, :, :, 8:32, :].reshape(ROWS, 128)
-        f_hi, f_lo = split2(flat)
+    def products(cells):
+        f_hi, f_lo = split2(cells.reshape(ROWS, 128))
         p_hi, p_lo = rows_hi[:, :ROWS], rows_lo[:, :ROWS]
         crossed = dot(p_hi, f_hi) + (dot(p_lo, f_hi) + dot(p_hi, f_lo))
         kept = crossed[3 * PROWS :]
         for q in range(3):
             kept = jnp.where(group == q, crossed[PROWS * q : PROWS * (q + 1)], kept)
-        by_slot = jnp.where(own_group, everywhere(kept), 0.0)
-        parts = split3(by_slot)
-        stacked = jnp.concatenate(parts + (jnp.zeros((PROWS, 128), BF16),), axis=0)
-        sums = dot(choose[...].astype(BF16), stacked)
-        grouped[k] = sums.reshape(BESIDE + 1, 8, 128)
-        copies = []
+        return everywhere(kept)
+
+    def group_sums(k, by_row):
+        stacked = jnp.concatenate(split2(jnp.where(own_group, by_row, 0.0)), axis=0)
+        grouped[k] = dot(choose[...].astype(BF16), stacked).reshape(BESIDE + 1, 8, 128)
+
+    def send_sums(k):
         for j, place in enumerate(targets):
-            copies.append(
-                pltpu.make_async_remote_copy(
-                    src_ref=grouped.at[k, j],
-                    dst_ref=partials.at[k, j],
-                    send_sem=sum_send.at[k],
-                    recv_sem=sum_recv.at[k],
-                    device_id=place,
-                    device_id_type=MESH,
-                )
-            )
-            copies[-1].start()
+            pltpu.make_async_remote_copy(
+                src_ref=grouped.at[k, j],
+                dst_ref=partials.at[k, j],
+                send_sem=sum_send.at[k],
+                recv_sem=sum_recv.at[k],
+                device_id=place,
+                device_id_type=MESH,
+            ).start()
 
     def halo_copies(k):
         own = field.at[k, :, :, pl.ds(8, CY), :]
@@ -249,6 +260,18 @@
             copy.start()
         return copies
 
+    def fill_overlap():
+        o_hi, o_lo = split2(proj[...])
+
+        def rows_by_rows(a, b):
+            return lax.dot_general(a, b, (((1,), (1,)), ((), ())), preferred_element_type=F32)
+
+        gram = rows_by_rows(o_hi, o_hi) + (rows_by_rows(o_hi, o_lo) + rows_by_rows(o_lo, o_hi))
+        g_hi, g_lo = split2(gram)
+        overlap[0] = g_hi
+        overlap[1] = g_lo
+
+    loads[4].wait()
     pot_pad[...] = jnp.zeros((128, 128), F32)
     pot_pad[: CZ * CX, :CY] = pot_ref[...]
     pot_t = pot_pad[...].T[:CY]
@@ -281,8 +304,6 @@
         total = total * factor[...]
         scaled[k] = total
         gathered[k, BESIDE] = total
-        for j in range(BESIDE + 1, 32):
-            gathered[k, j] = jnp.zeros((8, 128), F32)
         for j, place in enumerate(targets):
             pltpu.make_async_remote_copy(
                 src_ref=scaled.at[k],
@@ -340,40 +361,61 @@
                     total = total + WEIGHT[d] * (line[at - d] + line[at + d])
                 local[zi, xi] = total
 
-    def nonlocal_part(k):
+    def scale_local(k):
+        if k > 0:
+            for zi in range(ZI):
+                for xi in range(XI):
+                    local[zi, xi] = 2.0 * local[zi, xi] - field[k - 1, zi, xi, 8:32, :]
+
+    def picked_rows(k):
         landed = gathered.at[k, pl.ds(0, BESIDE)]
         pltpu.make_async_copy(landed, landed, spread_recv.at[k]).wait()
-        around = gathered[k].reshape(256, 128)
-        hot = pick[...].astype(BF16)
-        a, b, c = split3(around)
-        picked = dot(hot, a) + (dot(hot, b) + dot(hot, c))
+        a, b = split2(gathered[k].reshape(256, 128))
+        hot = pick[...]
+        picked = dot(hot, a) + dot(hot, b)
         rep = everywhere(jnp.where(own_group, picked, 0.0))
+        return rep if k == 0 else 2.0 * rep
+
+    def projected(rep):
+        r_hi, r_lo = split2(rep)
+        return dot(overlap[0], r_hi) + (dot(overlap[1], r_hi) + dot(overlap[0], r_lo))
+
+    def nonlocal_part(rep):
         blocks = jnp.concatenate([jnp.where(group == q, rep, 0.0) for q in range(4)], axis=0)
         b_hi, b_lo = split2(blocks)
         return dot(columns[...], jnp.concatenate([b_hi, b_hi, b_lo], axis=0))
 
-    started = []
+    group_sums(0, products(field[0, :, :, 8:32, :]))
+    pl.semaphore_wait(barrier, BESIDE)
+    send_sums(0)
+    copies = send_halos(0)
+    started = list(copies)
+    fill_diagonal()
+    fill_columns()
+    fill_overlap()
     for k in range(DEGREE):
-        send_sums(k)
-        copies = send_halos(k)
-        started += copies
-        if k == 0:
-            fill_diagonal()
-            fill_columns()
         send_atoms(k)
         stencil(k, copies)
-        returned = nonlocal_part(k).reshape(ZI, XI, CY, 128)
+        scale_local(k)
+        if k < DEGREE - 1:
+            ready = products(local[...])
+        rep = picked_rows(k)
+        if k < DEGREE - 1:
+            group_sums(k + 1, ready + projected(rep))
+            send_sums(k + 1)
+        returned = nonlocal_part(rep).reshape(ZI, XI, CY, 128)
         for zi in range(ZI):
             for xi in range(XI):
                 value = local[zi, xi] + returned[zi, xi]
-                if k > 0:
-                    value = 2.0 * value - field[k - 1, zi, xi, 8:32, :]
                 if k < DEGREE - 1:
                     field[k + 1, zi, xi, 8:32, :] = value
                 else:
                     for q in range(4):
                         zb, xb = q // 2, q % 2
                         out_ref[zb * ZI + zi, xb * XI + xi] = value[:, 32 * q : 32 * q + 32]
+        if k < DEGREE - 1:
+            copies = send_halos(k + 1)
+            started += copies
 
     for copy in started:
         copy.wait_send()
@@ -385,18 +427,20 @@
 
 def shards(sizes, orbitals, potential, projectors, targets, coupling):
     cells = orbitals.transpose(1, 2, 3, 0)
-    any_space = pl.BlockSpec(memory_space=pl.ANY)
+    hbm = pl.BlockSpec(memory_space=pl.ANY)
     vmem = pl.BlockSpec(memory_space=pltpu.VMEM)
-    smem = pl.BlockSpec(memory_space=pltpu.SMEM)
     steps = DEGREE
     result = pl.pallas_call(
         functools.partial(kernel, sizes),
         out_shape=jax.ShapeDtypeStruct((CZ, CX, CY, NORB), F32),
-        in_specs=[any_space, vmem, any_space, smem, smem],
+        in_specs=[hbm] * 5,
         out_specs=vmem,
         scratch_shapes=[
             pltpu.VMEM((CZ, CX, CY, NORB), F32),
             pltpu.VMEM((PROWS, CZ * CX * CY), F32),
+            pltpu.VMEM((CZ * CX, CY), F32),
+            pltpu.SMEM((SLOTS,), jnp.int32),
+            pltpu.SMEM((ATOM_DEV * NPJ,), F32),
             pltpu.VMEM((steps, ZI, XI, CY + 16, 128), F32),
             pltpu.VMEM((steps, ZI, XI, CY, 128), F32),
             pltpu.VMEM((steps, ZI, XI, CY, 128), F32),
@@ -414,13 +458,14 @@
             pltpu.VMEM((4 * PROWS, 384), BF16),
             pltpu.VMEM((4 * PROWS, 384), BF16),
             pltpu.VMEM((ROWS, 768), BF16),
-            pltpu.VMEM((8 * (BESIDE + 1), 256), F32),
-            pltpu.VMEM((PROWS, 256), F32),
+            pltpu.VMEM((8 * (BESIDE + 1), 128), F32),
+            pltpu.VMEM((PROWS, 256), BF16),
+            pltpu.VMEM((2, PROWS, PROWS), BF16),
             pltpu.VMEM((8, 128), F32),
             pltpu.VMEM((ZI, XI, CY, 128), F32),
             pltpu.VMEM((128, 128), F32),
             pltpu.VMEM((ZI, XI, CY, 128), F32),
-            pltpu.SemaphoreType.DMA((2,)),
+            pltpu.SemaphoreType.DMA((5,)),
             pltpu.SemaphoreType.DMA((steps, 8)),
             pltpu.SemaphoreType.DMA((steps, 8)),
             pltpu.SemaphoreType.DMA((steps,)),
@@ -429,7 +474,7 @@
             pltpu.SemaphoreType.DMA((steps,)),
         ],
         compiler_params=pltpu.CompilerParams(
-            collective_id=0, has_side_effects=True, vmem_limit_bytes=40 * 1024 * 1024
+            collective_id=0, has_side_effects=True, vmem_limit_bytes=60 * 1024 * 1024
         ),
     )(
         cells,

time: 79.7 us -> 76.9 us (0.965)
  local copies, waits for them, and re-layouts: 4.25 us -> 1.92 us
    unnamed x11 -> x1, local copies, waits for them, and re-layouts: 4.25 us -> 1.92 us
where the time goes in v2:
time: 76.9 us; the launch traced here: 76.7 us
  Pallas kernels  74.8 us (97%)
  local copies, waits for them, and re-layouts  1.92 us (2%)
    pallas_call x1, Pallas kernels, shards(): pl.pallas_call(functools.partial(kernel, sizes), out_shape=jax.ShapeDtype...  74.8 us
    unnamed x1, local copies, waits for them, and re-layouts  1.92 us

profile of v2, /device:TPU:1, one launch (start us, length us, event | category | flops | bytes accessed | tf_op | source)
XLA Modules:
  0.0 76.7 jit_solution(3201604425801333920)
XLA Ops:
  0.0 74.8 %shard_map.55 = f32[6,8,24,32]{3,2,1,0:T(8,128)} custom-call(f32[6,8,24,32]{3,2,1,0:T(8,128)} %bitcast.7, f32[48,24]{1,0:T(8,128)} %bitcast.9, f32[64,1152]{1,0:T(8,128)} %bitcast.8, s32[16]{0:T(128)} %bitcast.10, f32[32]{0:T(128)} %bitcast.11), custom_call_target="tpu_custom_call" | custom-call | tf_op jit(solution)/shard_map/pallas_call | solution.py:433
  74.8 1.9 %copy.7 = f32[32,6,8,24]{0,3,2,1:T(8,128)} copy(f32[32,6,8,24]{0,3,2,1:T(8,128)} %bitcast.6) | data formatting | bytes 294912

commit v3 on v2

--- a/solution.py
+++ b/solution.py
@@ -41,6 +41,26 @@
     if (a, b, c) != (1, 1, 1)
 ]
 BESIDE = len(OFFSETS)
+RUN = 8
+
+
+def pick_place(gz, gx, runs, inverse):
+    run, y, core = gz // RUN, lax.rem(gz, RUN), lax.rem(gx, 2)
+    last = runs - 1
+    step = -1 if inverse else 1
+    at_end, at_start = y == RUN - 1, y == 0
+    upper, lower = core == 1, core == 0
+    low, high = run == 0, run == last
+    if inverse:
+        shift_up, shift_down = at_end & upper & ~low, at_start & lower & ~high
+        wrap_up, wrap_down = at_end & lower & low, at_start & upper & high
+    else:
+        shift_up, shift_down = at_end & upper & ~high, at_start & lower & ~low
+        wrap_up, wrap_down = at_end & lower & high, at_start & upper & low
+    moved = jnp.where(shift_up | wrap_down, 1, 0) + jnp.where(shift_down | wrap_up, 1, 0)
+    runs_on = jnp.where(shift_up, step, jnp.where(shift_down, -step, 0))
+    runs_on = jnp.where(wrap_up, -step * last, jnp.where(wrap_down, step * last, runs_on))
+    return gz + RUN * runs_on, moved
 
 
 def split2(value):
@@ -103,6 +123,7 @@
     pick,
     overlap,
     factor,
+    guest_factor,
     diagonal,
     pot_pad,
     local,
@@ -113,6 +134,7 @@
     sum_recv,
     spread_send,
     spread_recv,
+    factor_sems,
 ):
     me = {name: lax.axis_index(name) for name in ("gz", "gx", "gy")}
 
@@ -123,11 +145,46 @@
         }
         return (place["gx"], place["gy"], place["gz"])
 
+    runs = sizes["gz"] // RUN
+
+    def host_of(place):
+        gz, moved = pick_place(place[2], place[0], runs, False)
+        return (place[0], place[1], gz), moved
+
     targets = [beside(offset) for offset in OFFSETS]
+    hosts = [host_of(place) for place in targets]
+    my_host, i_moved = host_of((me["gx"], me["gy"], me["gz"]))
+    guest_gz, hosting = pick_place(me["gz"], me["gx"], runs, True)
+    guest = (me["gx"], me["gy"], guest_gz)
+    around_guest = [
+        tuple(
+            lax.rem(at + step + sizes[name], sizes[name])
+            for name, at, step in zip(("gx", "gy", "gz"), guest, (offset[1], offset[2], offset[0]))
+        )
+        for offset in OFFSETS
+    ]
 
     barrier = pltpu.get_barrier_semaphore()
-    for place in targets:
+
+    def greet(place):
         pl.semaphore_signal(barrier, inc=1, device_id=place, device_id_type=MESH)
+
+    greeted = 27 * hosting + i_moved
+    for offset, place, (host, moved) in zip(OFFSETS, targets, hosts):
+        direct = 1 if sum(map(abs, offset)) == 1 else 1 - i_moved * moved
+        greeted = greeted + moved + direct
+        if isinstance(direct, int):
+            greet(place)
+        else:
+            pl.when(direct == 1)(functools.partial(greet, place))
+        pl.when(moved == 1)(functools.partial(greet, host))
+    pl.when(i_moved == 1)(functools.partial(greet, my_host))
+
+    @pl.when(hosting == 1)
+    def _():
+        greet(guest)
+        for place in around_guest:
+            greet(place)
 
     loads = [
         pltpu.make_async_copy(source, target, in_sems.at[i])
@@ -216,27 +273,51 @@
         grouped[k] = dot(choose[...].astype(BF16), stacked).reshape(BESIDE + 1, 8, 128)
 
     def send_sums(k):
-        for j, place in enumerate(targets):
+        for j, (place, moved) in enumerate(hosts):
             pltpu.make_async_remote_copy(
                 src_ref=grouped.at[k, j],
-                dst_ref=partials.at[k, j],
-                send_sem=sum_send.at[k],
-                recv_sem=sum_recv.at[k],
+                dst_ref=partials.at[k, j + BESIDE * moved],
+                send_sem=sum_send.at[k, 0],
+                recv_sem=sum_recv.at[k, moved],
                 device_id=place,
                 device_id_type=MESH,
             ).start()
 
+        @pl.when(i_moved == 1)
+        def _():
+            own_sums(k).start()
+
+    def own_sums(k):
+        return pltpu.make_async_remote_copy(
+            src_ref=grouped.at[k, BESIDE],
+            dst_ref=partials.at[k, 2 * BESIDE],
+            send_sem=sum_send.at[k, 1],
+            recv_sem=sum_recv.at[k, 1],
+            device_id=my_host,
+            device_id_type=MESH,
+        )
+
+    def send_factor():
+        return pltpu.make_async_remote_copy(
+            src_ref=factor,
+            dst_ref=guest_factor,
+            send_sem=factor_sems.at[0],
+            recv_sem=factor_sems.at[1],
+            device_id=my_host,
+            device_id_type=MESH,
+        )
+
     def halo_copies(k):
         own = field.at[k, :, :, pl.ds(8, CY), :]
         moves = (
+            (own, z_low.at[k], (1, 0, 0)),
+            (own, z_high.at[k], (-1, 0, 0)),
+            (field.at[k, :, :, pl.ds(24, 8), :], field.at[k, :, :, pl.ds(0, 8), :], (0, 0, 1)),
+            (field.at[k, :, :, pl.ds(8, 8), :], field.at[k, :, :, pl.ds(32, 8), :], (0, 0, -1)),
             (field.at[k, :, pl.ds(2, 2), pl.ds(8, CY), :], x_low.at[k], (0, 1, 0)),
             (field.at[k, :, pl.ds(0, 2), pl.ds(8, CY), :], x_high.at[k], (0, -1, 0)),
             (send_low_part.at[k], x_low_part.at[k], (0, 1, 0)),
             (send_high_part.at[k], x_high_part.at[k], (0, -1, 0)),
-            (own, z_low.at[k], (1, 0, 0)),
-            (own, z_high.at[k], (-1, 0, 0)),
-            (field.at[k, :, :, pl.ds(24, 8), :], field.at[k, :, :, pl.ds(0, 8), :], (0, 0, 1)),
-            (field.at[k, :, :, pl.ds(8, 8), :], field.at[k, :, :, pl.ds(32, 8), :], (0, 0, -1)),
         )
         return [
             pltpu.make_async_remote_copy(
@@ -296,23 +377,43 @@
         columns[:, 256:512] = t_lo
         columns[:, 512:768] = t_hi
 
+    def spread(k, which, place, slot):
+        return pltpu.make_async_remote_copy(
+            src_ref=scaled.at[k, which],
+            dst_ref=gathered.at[k, slot],
+            send_sem=spread_send.at[k, which],
+            recv_sem=spread_recv.at[k, 0 if slot < BESIDE else 1],
+            device_id=place,
+            device_id_type=MESH,
+        )
+
     def send_atoms(k):
-        pltpu.make_async_copy(partials.at[k], partials.at[k], sum_recv.at[k]).wait()
-        total = grouped[k, BESIDE]
-        for j in range(BESIDE):
-            total = total + partials[k, j]
-        total = total * factor[...]
-        scaled[k] = total
-        gathered[k, BESIDE] = total
-        for j, place in enumerate(targets):
-            pltpu.make_async_remote_copy(
-                src_ref=scaled.at[k],
-                dst_ref=gathered.at[k, BESIDE - 1 - j],
-                send_sem=spread_send.at[k],
-                recv_sem=spread_recv.at[k],
-                device_id=place,
-                device_id_type=MESH,
-            ).start()
+        @pl.when(i_moved == 0)
+        def _():
+            landed = partials.at[k, pl.ds(0, BESIDE)]
+            pltpu.make_async_copy(landed, landed, sum_recv.at[k, 0]).wait()
+            total = grouped[k, BESIDE]
+            for j in range(BESIDE):
+                total = total + partials[k, j]
+            total = total * factor[...]
+            scaled[k, 0] = total
+            for j, place in enumerate(targets):
+                spread(k, 0, place, BESIDE - 1 - j).start()
+            gathered[k, BESIDE] = total
+
+        @pl.when(hosting == 1)
+        def _():
+            landed = partials.at[k, pl.ds(BESIDE, BESIDE + 1)]
+            pltpu.make_async_copy(landed, landed, sum_recv.at[k, 1]).wait()
+            if k == 0:
+                send_factor().wait_recv()
+            total = partials[k, 2 * BESIDE]
+            for j in range(BESIDE, 2 * BESIDE):
+                total = total + partials[k, j]
+            scaled[k, 1] = total * guest_factor[...]
+            for j, place in enumerate(around_guest):
+                spread(k, 1, place, BESIDE - 1 - j).start()
+            spread(k, 1, guest, BESIDE).start()
 
     def stencil(k, copies):
         for copy in copies:
@@ -369,7 +470,13 @@
 
     def picked_rows(k):
         landed = gathered.at[k, pl.ds(0, BESIDE)]
-        pltpu.make_async_copy(landed, landed, spread_recv.at[k]).wait()
+        pltpu.make_async_copy(landed, landed, spread_recv.at[k, 0]).wait()
+
+        @pl.when(i_moved == 1)
+        def _():
+            own = gathered.at[k, BESIDE]
+            pltpu.make_async_copy(own, own, spread_recv.at[k, 1]).wait()
+
         a, b = split2(gathered[k].reshape(256, 128))
         hot = pick[...]
         picked = dot(hot, a) + dot(hot, b)
@@ -386,8 +493,13 @@
         return dot(columns[...], jnp.concatenate([b_hi, b_hi, b_lo], axis=0))
 
     group_sums(0, products(field[0, :, :, 8:32, :]))
-    pl.semaphore_wait(barrier, BESIDE)
+    pl.semaphore_wait(barrier, greeted)
     send_sums(0)
+
+    @pl.when(i_moved == 1)
+    def _():
+        send_factor().start()
+
     copies = send_halos(0)
     started = list(copies)
     fill_diagonal()
@@ -421,8 +533,24 @@
         copy.wait_send()
     for k in range(DEGREE):
         sent = grouped.at[k, pl.ds(0, BESIDE)]
-        pltpu.make_async_copy(sent, sent, sum_send.at[k]).wait()
-        pltpu.make_async_copy(sent, sent, spread_send.at[k]).wait()
+        pltpu.make_async_copy(sent, sent, sum_send.at[k, 0]).wait()
+
+        @pl.when(i_moved == 0)
+        def _():
+            pltpu.make_async_copy(sent, sent, spread_send.at[k, 0]).wait()
+
+        @pl.when(i_moved == 1)
+        def _():
+            own_sums(k).wait_send()
+
+        @pl.when(hosting == 1)
+        def _():
+            whole = grouped.at[k]
+            pltpu.make_async_copy(whole, whole, spread_send.at[k, 1]).wait()
+
+    @pl.when(i_moved == 1)
+    def _():
+        send_factor().wait_send()
 
 
 def shards(sizes, orbitals, potential, projectors, targets, coupling):
@@ -451,8 +579,8 @@
             pltpu.VMEM((steps, ZI, CY, 128), F32),
             pltpu.VMEM((steps, ZI, CY, 128), F32),
             pltpu.VMEM((steps, BESIDE + 1, 8, 128), F32),
-            pltpu.VMEM((steps, BESIDE, 8, 128), F32),
-            pltpu.VMEM((steps, 8, 128), F32),
+            pltpu.VMEM((steps, 2 * BESIDE + 1, 8, 128), F32),
+            pltpu.VMEM((steps, 2, 8, 128), F32),
             pltpu.VMEM((steps, 32, 8, 128), F32),
             pltpu.VMEM((4 * PROWS, 384), F32),
             pltpu.VMEM((4 * PROWS, 384), BF16),
@@ -462,16 +590,18 @@
             pltpu.VMEM((PROWS, 256), BF16),
             pltpu.VMEM((2, PROWS, PROWS), BF16),
             pltpu.VMEM((8, 128), F32),
+            pltpu.VMEM((8, 128), F32),
             pltpu.VMEM((ZI, XI, CY, 128), F32),
             pltpu.VMEM((128, 128), F32),
             pltpu.VMEM((ZI, XI, CY, 128), F32),
             pltpu.SemaphoreType.DMA((5,)),
             pltpu.SemaphoreType.DMA((steps, 8)),
             pltpu.SemaphoreType.DMA((steps, 8)),
-            pltpu.SemaphoreType.DMA((steps,)),
-            pltpu.SemaphoreType.DMA((steps,)),
-            pltpu.SemaphoreType.DMA((steps,)),
-            pltpu.SemaphoreType.DMA((steps,)),
+            pltpu.SemaphoreType.DMA((steps, 2)),
+            pltpu.SemaphoreType.DMA((steps, 2)),
+            pltpu.SemaphoreType.DMA((steps, 2)),
+            pltpu.SemaphoreType.DMA((steps, 2)),
+            pltpu.SemaphoreType.DMA((2,)),
         ],
         compiler_params=pltpu.CompilerParams(
             collective_id=0, has_side_effects=True, vmem_limit_bytes=60 * 1024 * 1024

time: 76.9 us -> 75.3 us (0.979)
  Pallas kernels: 74.8 us -> 73.2 us
    pallas_call x1, Pallas kernels: 74.8 us -> 73.2 us  [shards(): pl.pallas_call(functools.partial(kernel, sizes), out_shape=jax.ShapeDtype...]
where the time goes in v3:
time: 75.3 us; the launch traced here: 75.1 us
  Pallas kernels  73.2 us (97%)
  local copies, waits for them, and re-layouts  1.92 us (3%)
    pallas_call x1, Pallas kernels, shards(): pl.pallas_call(functools.partial(kernel, sizes), out_shape=jax.ShapeDtype...  73.2 us
    unnamed x1, local copies, waits for them, and re-layouts  1.92 us

profile of v3, /device:TPU:1, one launch (start us, length us, event | category | flops | bytes accessed | tf_op | source)
XLA Modules:
  0.0 75.1 jit_solution(4619435122337129940)
XLA Ops:
  0.0 73.2 %shard_map.55 = f32[6,8,24,32]{3,2,1,0:T(8,128)} custom-call(f32[6,8,24,32]{3,2,1,0:T(8,128)} %bitcast.7, f32[48,24]{1,0:T(8,128)} %bitcast.9, f32[64,1152]{1,0:T(8,128)} %bitcast.8, s32[16]{0:T(128)} %bitcast.10, f32[32]{0:T(128)} %bitcast.11), custom_call_target="tpu_custom_call" | custom-call | tf_op jit(solution)/shard_map/pallas_call | solution.py:561
  73.2 1.9 %copy.7 = f32[32,6,8,24]{0,3,2,1:T(8,128)} copy(f32[32,6,8,24]{0,3,2,1:T(8,128)} %bitcast.6) | data formatting | bytes 294912

commit v4 on v3

--- a/solution.py
+++ b/solution.py
@@ -337,7 +337,7 @@
             send_low_part[k, zi] = jnp.where(is_x1, cell[1], roll(cell[0], 96))
             send_high_part[k, zi] = jnp.where(is_x1, roll(cell[2], 32), cell[3])
         copies = halo_copies(k)
-        for copy in copies:
+        for copy in copies[2:]:
             copy.start()
         return copies
 
@@ -387,7 +387,11 @@
             device_id_type=MESH,
         )
 
-    def send_atoms(k):
+    def send_atoms(k, copies):
+        for copy in copies[2:4]:
+            copy.wait_recv()
+        for copy in copies[:2]:
+            copy.start()
         @pl.when(i_moved == 0)
         def _():
             landed = partials.at[k, pl.ds(0, BESIDE)]
@@ -416,7 +420,7 @@
             spread(k, 1, guest, BESIDE).start()
 
     def stencil(k, copies):
-        for copy in copies:
+        for copy in copies[:2] + copies[4:]:
             copy.wait_recv()
         for xi in range(XI):
             own = [field[k, zi, xi, 8:32, :] for zi in range(ZI)]
@@ -506,7 +510,7 @@
     fill_columns()
     fill_overlap()
     for k in range(DEGREE):
-        send_atoms(k)
+        send_atoms(k, copies)
         stencil(k, copies)
         scale_local(k)
         if k < DEGREE - 1:

time: 75.3 us -> 72.1 us (0.958)
  Pallas kernels: 73.2 us -> 70 us
    pallas_call x1, Pallas kernels: 73.2 us -> 70 us  [shards(): pl.pallas_call(functools.partial(kernel, sizes), out_shape=jax.ShapeDtype...]
where the time goes in v4:
time: 72.1 us; the launch traced here: 71.9 us
  Pallas kernels  70 us (97%)
  local copies, waits for them, and re-layouts  1.92 us (3%)
    pallas_call x1, Pallas kernels, shards(): pl.pallas_call(functools.partial(kernel, sizes), out_shape=jax.ShapeDtype...  70 us
    unnamed x1, local copies, waits for them, and re-layouts  1.92 us

profile of v4, /device:TPU:1, one launch (start us, length us, event | category | flops | bytes accessed | tf_op | source)
XLA Modules:
  0.0 71.9 jit_solution(8516106479204245935)
XLA Ops:
  0.0 70.0 %shard_map.55 = f32[6,8,24,32]{3,2,1,0:T(8,128)} custom-call(f32[6,8,24,32]{3,2,1,0:T(8,128)} %bitcast.7, f32[48,24]{1,0:T(8,128)} %bitcast.9, f32[64,1152]{1,0:T(8,128)} %bitcast.8, s32[16]{0:T(128)} %bitcast.10, f32[32]{0:T(128)} %bitcast.11), custom_call_target="tpu_custom_call" | custom-call | tf_op jit(solution)/shard_map/pallas_call | solution.py:565
  70.0 1.9 %copy.7 = f32[32,6,8,24]{0,3,2,1:T(8,128)} copy(f32[32,6,8,24]{0,3,2,1:T(8,128)} %bitcast.6) | data formatting | bytes 294912

commit v5 on v4

--- a/solution.py
+++ b/solution.py
@@ -75,6 +75,13 @@
     mid = rest.astype(BF16)
     low = (rest - mid.astype(F32)).astype(BF16)
     return high, mid, low
+
+
+def in_pairs(values):
+    while len(values) > 1:
+        paired = [a + b for a, b in zip(values[::2], values[1::2])]
+        values = paired + values[len(paired) * 2 :]
+    return values[0]
 
 
 def dot(a, b):
@@ -120,6 +127,7 @@
     rows_lo,
     columns,
     choose,
+    choose_half,
     pick,
     overlap,
     factor,
@@ -240,6 +248,8 @@
     atom_row = lax.broadcasted_iota(jnp.int32, (8, 128), 0)
     for j in range(BESIDE + 1):
         choose[8 * j : 8 * j + 8, :] = jnp.where(named_lane == atom_row + 8 * j, 1.0, 0.0)
+    choose[8 * (BESIDE + 1) :, :] = jnp.zeros((8, 128), F32)
+    choose_half[...] = choose[...].astype(BF16)
     pick[...] = jnp.where(named_row == lanes_of((PROWS, 256)), 1.0, 0.0).astype(BF16)
     for k in range(DEGREE):
         for j in range(BESIDE + 1, 32):
@@ -270,7 +280,8 @@
 
     def group_sums(k, by_row):
         stacked = jnp.concatenate(split2(jnp.where(own_group, by_row, 0.0)), axis=0)
-        grouped[k] = dot(choose[...].astype(BF16), stacked).reshape(BESIDE + 1, 8, 128)
+        sums = dot(choose_half[...], stacked)
+        grouped[k] = sums[: 8 * (BESIDE + 1)].reshape(BESIDE + 1, 8, 128)
 
     def send_sums(k):
         for j, (place, moved) in enumerate(hosts):
@@ -388,17 +399,14 @@
         )
 
     def send_atoms(k, copies):
-        for copy in copies[2:4]:
-            copy.wait_recv()
-        for copy in copies[:2]:
+        for behind, copy in zip(copies[2:4], copies[:2]):
+            behind.wait_recv()
             copy.start()
         @pl.when(i_moved == 0)
         def _():
             landed = partials.at[k, pl.ds(0, BESIDE)]
             pltpu.make_async_copy(landed, landed, sum_recv.at[k, 0]).wait()
-            total = grouped[k, BESIDE]
-            for j in range(BESIDE):
-                total = total + partials[k, j]
+            total = in_pairs([grouped[k, BESIDE]] + [partials[k, j] for j in range(BESIDE)])
             total = total * factor[...]
             scaled[k, 0] = total
             for j, place in enumerate(targets):
@@ -411,9 +419,7 @@
             pltpu.make_async_copy(landed, landed, sum_recv.at[k, 1]).wait()
             if k == 0:
                 send_factor().wait_recv()
-            total = partials[k, 2 * BESIDE]
-            for j in range(BESIDE, 2 * BESIDE):
-                total = total + partials[k, j]
+            total = in_pairs([partials[k, j] for j in range(BESIDE, 2 * BESIDE + 1)])
             scaled[k, 1] = total * guest_factor[...]
             for j, place in enumerate(around_guest):
                 spread(k, 1, place, BESIDE - 1 - j).start()
@@ -590,7 +596,8 @@
             pltpu.VMEM((4 * PROWS, 384), BF16),
             pltpu.VMEM((4 * PROWS, 384), BF16),
             pltpu.VMEM((ROWS, 768), BF16),
-            pltpu.VMEM((8 * (BESIDE + 1), 128), F32),
+            pltpu.VMEM((8 * (BESIDE + 2), 128), F32),
+            pltpu.VMEM((8 * (BESIDE + 2), 128), BF16),
             pltpu.VMEM((PROWS, 256), BF16),
             pltpu.VMEM((2, PROWS, PROWS), BF16),
             pltpu.VMEM((8, 128), F32),

time: 72.1 us -> 72.9 us (1.011)
  no operation moved by 1% of the time
where the time goes in v5:
time: 72.9 us; the launch traced here: 72 us
  Pallas kernels  70.1 us (96%)
  local copies, waits for them, and re-layouts  1.92 us (3%)
    pallas_call x1, Pallas kernels, shards(): pl.pallas_call(functools.partial(kernel, sizes), out_shape=jax.ShapeDtype...  70.1 us
    unnamed x1, local copies, waits for them, and re-layouts  1.92 us

profile of v5, /device:TPU:1, one launch (start us, length us, event | category | flops | bytes accessed | tf_op | source)
XLA Modules:
  0.0 72.0 jit_solution(3218412284911784554)
XLA Ops:
  0.0 70.1 %shard_map.55 = f32[6,8,24,32]{3,2,1,0:T(8,128)} custom-call(f32[6,8,24,32]{3,2,1,0:T(8,128)} %bitcast.7, f32[48,24]{1,0:T(8,128)} %bitcast.9, f32[64,1152]{1,0:T(8,128)} %bitcast.8, s32[16]{0:T(128)} %bitcast.10, f32[32]{0:T(128)} %bitcast.11), custom_call_target="tpu_custom_call" | custom-call | tf_op jit(solution)/shard_map/pallas_call | solution.py:571
  70.1 1.9 %copy.7 = f32[32,6,8,24]{0,3,2,1:T(8,128)} copy(f32[32,6,8,24]{0,3,2,1:T(8,128)} %bitcast.6) | data formatting | bytes 294912
